TPU v7x, 512 devices: a whole 4x8x8 slice. The times are simulated.
512 devices in a mesh: chan: 8 (over y_hi, x), row: 64 (over z, y_lo, core).
Axes of the slice: x: 4, y: 8 (y_hi: 2, y_lo: 4; y = y_hi * 4 + y_lo), z: 8, core: 2. Of those that a mesh axis runs over, the one named last changes fastest.
Arguments:
- inputs: bfloat16 [1, 192, 448, 1024], P(None, 'row', None, 'chan'), may hold values from -6 to 6
- cotangent: bfloat16 [1, 192, 448, 1024], P(None, 'row', None, 'chan'), may hold values from -6 to 6
- ln_gain: float32 [1024], P('chan'), may hold values from 0.1 to 1.9
- ln_shift: float32 [1024], P('chan'), may hold values from -3 to 3
- first_weight: bfloat16 [2, 1024, 128], P(None, 'chan'), may hold values from -0.375 to 0.375
- first_bias: float32 [2, 1024], P(None, 'chan'), may hold values from -3 to 3
- second_weight: bfloat16 [2, 1024, 128], P(None, 'chan'), may hold values from -0.375 to 0.375
- second_bias: float32 [2, 1024], P(None, 'chan'), may hold values from -3 to 3
Outputs:
- input_grad: bfloat16 [1, 192, 448, 1024], P(None, 'row', None, 'chan')
- first_weight_grad: float32 [2, 1024, 128], P(None, 'chan')
- first_bias_grad: float32 [2, 1024], P(None, 'chan')
- second_weight_grad: float32 [2, 1024, 128], P(None, 'chan')
- second_bias_grad: float32 [2, 1024], P(None, 'chan')
- gain_grad: float32 [1024], P('chan')
- shift_grad: float32 [1024], P('chan')
All inputs are finite; a program needn't handle non-finite values.
Results may differ from a plain program's by a relative error of at most 0.03.
The roundings to bfloat16 on the way count: a program that leaves them out, or rounds other values in their place, can miss the bound.
Values sent between devices are 32-bit elements; how exact they have to be, the bound alone decides.
A program may use at most 64 MiB of HBM per device.

v0:
```python
import math

import jax
import jax.numpy as jnp
from jax import lax
from jax.sharding import PartitionSpec as P

H = 192
K = 192
BS = 128


EPS = 1e-05
LAMBDA = 0.01
HIGHER = lax.Precision.HIGH
ROOT_TWO_PI = math.sqrt(2.0 / math.pi)


def gelu_parts(values):
    inner = ROOT_TWO_PI * (values + 0.044715 * values * values * values)
    tangent = jnp.tanh(inner)
    output = 0.5 * values * (1.0 + tangent)
    slope = 0.5 * (1.0 + tangent) + 0.5 * values * (1.0 - tangent * tangent) * ROOT_TWO_PI * (
        1.0 + 3.0 * 0.044715 * values * values
    )
    return (output, slope)


def shrink_slope(values):
    tangent = jnp.tanh(values / LAMBDA)
    return tangent * tangent


def lon_table(width, kept):
    column = jnp.arange(width, dtype=jnp.int32)[:, None]
    number = jnp.arange(kept, dtype=jnp.int32)[None, :]
    phase = (column * number % width).astype(jnp.float32) * (2.0 * math.pi / width)
    factor = 1.0 / math.sqrt(width)
    return jnp.stack([jnp.cos(phase) * factor, -jnp.sin(phase) * factor], axis=1)


def lat_table(length, sign):
    first = jnp.arange(length, dtype=jnp.int32)[:, None]
    second = jnp.arange(length, dtype=jnp.int32)[None, :]
    phase = (first * second % length).astype(jnp.float32) * (2.0 * math.pi / length)
    factor = 1.0 / math.sqrt(length)
    cosine = jnp.cos(phase) * factor
    sine = jnp.sin(phase) * factor * -sign
    return jnp.stack([jnp.stack([cosine, sine], 1), jnp.stack([-sine, cosine], 1)], 0)


def mult(left, right):
    return jnp.einsum("bgkni,nio->bgkno", left, right, preferred_element_type=jnp.float32)


def mult_t(left, right):
    return jnp.einsum("bgkno,nio->bgkni", left, right, preferred_element_type=jnp.float32)


def outer(left, right):
    return jnp.einsum("bgkni,bgkno->nio", left, right, preferred_element_type=jnp.float32)


def on_device(
    inputs, cotangent, ln_gain, ln_shift, first_weight, first_bias, second_weight, second_bias
):
    batch, rows, width, local = inputs.shape
    blocks = local // BS
    total_chan = local * lax.axis_size("chan")
    values = inputs.astype(jnp.float32)
    mean = lax.psum(jnp.sum(values, -1), "chan") / total_chan
    centred = values - mean[..., None]
    variance = lax.psum(jnp.sum(centred * centred, -1), "chan") / total_chan
    rstd = lax.rsqrt(variance + EPS)[..., None]
    normed = centred * rstd
    mixed_in = normed * ln_gain + ln_shift
    longitude = lon_table(width, K)
    table_high = longitude.astype(jnp.bfloat16)
    table_low = (longitude - table_high.astype(jnp.float32)).astype(jnp.bfloat16)
    kept = jnp.where(jnp.arange(K) == 0, 1.0, 2.0).astype(jnp.float32)
    forward_lat = lat_table(H, -1)
    inverse_lat = lat_table(H, 1)

    def to_spectrum(piece):
        return jnp.einsum("qgph,bhpkc->bqgkc", forward_lat, piece, precision=HIGHER)

    input_lon = jnp.einsum("bhwc,wpk->bhpkc", mixed_in, longitude, precision=HIGHER)
    high = jnp.einsum("bhwc,wpk->bhpkc", cotangent, table_high, preferred_element_type=jnp.float32)
    low = jnp.einsum("bhwc,wpk->bhpkc", cotangent, table_low, preferred_element_type=jnp.float32)
    cot_lon = (high + low) * kept[None, None, None, :, None]
    spectrum = to_spectrum(
        lax.all_to_all(input_lon, "row", split_axis=3, concat_axis=1, tiled=True)
    )
    cot_spec = to_spectrum(lax.all_to_all(cot_lon, "row", split_axis=3, concat_axis=1, tiled=True))
    kept_local = spectrum.shape[3]
    block_shape = (batch, 2, H, kept_local, blocks, BS)
    w_one = first_weight.reshape(2, blocks, BS, BS)
    w_two = second_weight.reshape(2, blocks, BS, BS)
    b_one = first_bias.reshape(2, blocks, BS)
    b_two = second_bias.reshape(2, blocks, BS)
    spec_blocks = spectrum.reshape(block_shape).astype(jnp.bfloat16)
    spec_re = spec_blocks[:, 0]
    spec_im = spec_blocks[:, 1]
    pre_one_re = mult(spec_re, w_one[0]) - mult(spec_im, w_one[1]) + b_one[0]
    pre_one_im = mult(spec_re, w_one[1]) + mult(spec_im, w_one[0]) + b_one[1]
    act_re, slope_re = gelu_parts(pre_one_re)
    act_im, slope_im = gelu_parts(pre_one_im)
    hid_re = act_re.astype(jnp.bfloat16)
    hid_im = act_im.astype(jnp.bfloat16)
    pre_two_re = mult(hid_re, w_two[0]) - mult(hid_im, w_two[1]) + b_two[0]
    pre_two_im = mult(hid_re, w_two[1]) + mult(hid_im, w_two[0]) + b_two[1]
    cot_blocks = cot_spec.reshape(block_shape)
    grad_two_re = (cot_blocks[:, 0] * shrink_slope(pre_two_re)).astype(jnp.bfloat16)
    grad_two_im = (cot_blocks[:, 1] * shrink_slope(pre_two_im)).astype(jnp.bfloat16)
    grad_hid_re = mult_t(grad_two_re, w_two[0]) + mult_t(grad_two_im, w_two[1])
    grad_hid_im = mult_t(grad_two_im, w_two[0]) - mult_t(grad_two_re, w_two[1])
    dw_two = jnp.stack(
        [
            outer(hid_re, grad_two_re) + outer(hid_im, grad_two_im),
            outer(hid_re, grad_two_im) - outer(hid_im, grad_two_re),
        ]
    )
    db_two = jnp.stack(
        [
            jnp.sum(grad_two_re.astype(jnp.float32), (0, 1, 2)),
            jnp.sum(grad_two_im.astype(jnp.float32), (0, 1, 2)),
        ]
    )
    grad_pre_re = (grad_hid_re * slope_re).astype(jnp.bfloat16)
    grad_pre_im = (grad_hid_im * slope_im).astype(jnp.bfloat16)
    dw_one = jnp.stack(
        [
            outer(spec_re, grad_pre_re) + outer(spec_im, grad_pre_im),
            outer(spec_re, grad_pre_im) - outer(spec_im, grad_pre_re),
        ]
    )
    db_one = jnp.stack(
        [
            jnp.sum(grad_pre_re.astype(jnp.float32), (0, 1, 2)),
            jnp.sum(grad_pre_im.astype(jnp.float32), (0, 1, 2)),
        ]
    )
    grad_spec_re = mult_t(grad_pre_re, w_one[0]) + mult_t(grad_pre_im, w_one[1])
    grad_spec_im = mult_t(grad_pre_im, w_one[0]) - mult_t(grad_pre_re, w_one[1])
    grad_spec = jnp.stack([grad_spec_re, grad_spec_im], 1).reshape(batch, 2, H, kept_local, local)
    grad_lat = jnp.einsum("phqg,bqgkc->bhpkc", inverse_lat, grad_spec, precision=HIGHER)
    grad_mixed = jnp.einsum(
        "bhpkc,wpk->bhwc",
        lax.all_to_all(grad_lat, "row", split_axis=1, concat_axis=3, tiled=True),
        longitude,
        precision=HIGHER,
    )
    grad_norm = grad_mixed * ln_gain
    sum_one, sum_two = lax.psum((jnp.sum(grad_norm, -1), jnp.sum(grad_norm * normed, -1)), "chan")
    cot_values = cotangent.astype(jnp.float32)
    input_grad = cot_values + rstd * (
        grad_norm - sum_one[..., None] / total_chan - normed * (sum_two[..., None] / total_chan)
    )
    gain_local = jnp.sum(grad_mixed * normed, (0, 1, 2))
    shift_local = jnp.sum(grad_mixed, (0, 1, 2))
    dw_one, db_one, dw_two, db_two, gain_total, shift_total = lax.psum(
        (dw_one, db_one, dw_two, db_two, gain_local, shift_local), "row"
    )
    spec_scale = 1.0 / math.sqrt(batch * H * K)
    ln_scale = 1.0 / math.sqrt(batch * H * width)
    return (
        input_grad.astype(jnp.bfloat16),
        (dw_one * spec_scale).reshape(2, local, BS),
        (db_one * spec_scale).reshape(2, local),
        (dw_two * spec_scale).reshape(2, local, BS),
        (db_two * spec_scale).reshape(2, local),
        gain_total * ln_scale,
        shift_total * ln_scale,
    )


def solution(mesh):
    placed = (
        P(None, "row", None, "chan"),
        P(None, "row", None, "chan"),
        P("chan"),
        P("chan"),
        P(None, "chan", None),
        P(None, "chan"),
        P(None, "chan", None),
        P(None, "chan"),
    )
    return jax.shard_map(
        on_device,
        mesh=mesh,
        in_specs=placed,
        out_specs=(
            P(None, "row", None, "chan"),
            P(None, "chan", None),
            P(None, "chan"),
            P(None, "chan", None),
            P(None, "chan"),
            P("chan"),
            P("chan"),
        ),
        check_vma=False,
    )
```

profile of v0, /device:TPU:32, one launch (start us, length us, event | category | flops | bytes accessed | tf_op | source)
XLA Modules:
  0.0 842.0 jit_solution(7422232751010336990)
XLA Ops:
  7.2 1.7 negate_multiply_fusion
  8.8 0.2 convert_reduce_fusion
  9.1 26.3 %psum.70 = f32[1,3,448]{2,1,0:T(4,128)S(1)} all-reduce(f32[1,3,448]{2,1,0:T(4,128)S(1)} %bitcast.439), channel_id=1, replica_groups=mesh['chan'=8,'row'=64] {'chan'}, use_global_device_ids=true, to_apply=%region_1.0 | all-reduce | flops 1344 | bytes 10752 | tf_op jit(solution)/shard_map/psum | solution.py:71
  35.4 0.5 fusion.63
  35.9 24.0 %psum.71 = f32[1,3,448]{2,1,0:T(4,128)S(1)} all-reduce(f32[1,3,448]{2,1,0:T(4,128)S(1)} %bitcast.440), channel_id=1, replica_groups=mesh['chan'=8,'row'=64] {'chan'}, use_global_device_ids=true, to_apply=%region_3.0 | all-reduce | flops 1344 | bytes 10752 | tf_op jit(solution)/shard_map/psum | solution.py:73
  60.0 0.6 copy-done.18
  60.7 1.1 convolution_bitcast_fusion.2
  61.8 1.3 copy.49
  63.0 14.5 %all-to-all-start.1 = ((f32[1,3,2,192,128]{4,2,1,0,3:T(2,128)}), f32[1,3,2,192,128]{4,2,1,0,3:T(2,128)S(1)}, u32[]{:S(2)}, u32[]{:S(2)}) async-start(f32[1,3,2,192,128]{4,2,1,0,3:T(2,128)} %copy.49), calls=%async_computation.1 | async-start | bytes 1179648 | tf_op jit(solution)/shard_map/all_to_all | solution.py:92
  77.5 0.4 fusion.77
  77.9 0.4 fusion.2
  78.3 1.3 copy.44
  79.6 0.8 fusion.142
  80.3 0.8 cosine_multiply_fusion.1
  81.2 0.8 fusion.107
  81.9 0.9 fusion.71
  82.9 0.5 slice_bitcast_fusion.14
  83.5 0.5 slice_bitcast_fusion.13
  84.1 13.1 %all-to-all-done.1 = f32[1,3,2,192,128]{4,2,1,0,3:T(2,128)S(1)} async-done(((f32[1,3,2,192,128]{4,2,1,0,3:T(2,128)}), f32[1,3,2,192,128]{4,2,1,0,3:T(2,128)S(1)}, u32[]{:S(2)}, u32[]{:S(2)}) %all-to-all-start.1) | async-done | bytes 589856 | tf_op jit(solution)/shard_map/all_to_all | solution.py:92
  97.1 5.6 all-to-all-start
  103.2 0.8 fusion.12
  104.2 0.9 fusion.139
  105.1 0.7 copy-done.21
  105.8 0.9 multiply_convert_fusion.1
  106.7 0.9 fusion.137
  107.8 14.3 %all-to-all-done = f32[1,3,2,192,128]{4,2,1,0,3:T(2,128)} async-done(((f32[1,3,2,192,128]{4,2,1,0,3:T(2,128)}), f32[1,3,2,192,128]{4,2,1,0,3:T(2,128)}, u32[]{:S(2)}, u32[]{:S(2)}) %all-to-all-start) | async-done | bytes 589856 | tf_op jit(solution)/shard_map/all_to_all | solution.py:94
  122.1 1.3 copy.45
  123.6 0.8 convolution_bitcast_fusion.3
  124.6 0.5 copy-done.20
  125.0 0.3 multiply_convert_fusion
  125.3 0.6 copy-done.5
  126.0 0.2 convert_reduce_fusion.1
  126.4 0.9 convolution_bitcast_fusion.6
  127.4 0.6 copy-done.14
  128.0 0.2 convert_reduce_fusion.2
  128.4 0.9 convolution_bitcast_fusion.4
  129.3 0.3 convert_reduce_fusion.3
  129.8 0.9 convolution_bitcast_fusion.10
  130.8 0.3 convert_reduce_fusion.4
  131.3 0.9 convolution_bitcast_fusion.8
  132.5 0.8 copy-done.2
  133.3 0.8 convolution_bitcast_fusion
  134.1 1.3 copy.54
  135.4 5.3 all-to-all-start.2
  140.7 0.2 fusion.40
  141.0 0.5 copy-done.10
  141.5 0.2 fusion.42
  141.8 0.7 pad_maximum_fusion.9
  142.6 0.2 fusion.36
  142.8 0.6 copy-done.12
  143.4 0.2 fusion.38
  143.7 0.7 pad_maximum_fusion.8
  144.4 496.3 %all-reduce.5.cloned.1.call-done = (f32[2,1,128,128]{3,2,1,0:T(8,128)}, f32[2,1,128,128]{3,2,1,0:T(8,128)}) async-done(((f32[2,1,128,128]{3,2,1,0:T(8,128)}, f32[2,1,128,128]{3,2,1,0:T(8,128)}), (f32[2,1,128,128]{3,2,1,0:T(8,128)}, f32[2,1,128,128]{3,2,1,0:T(8,128)})) %all-reduce.5.cloned.1.call-update) | async-done | bytes 262160 | tf_op jit(solution)/shard_map/psum | solution.py:161
  640.7 1.6 multiply_bitcast_fusion
  642.3 0.7 multiply_bitcast_fusion.1
  643.2 0.6 copy-done.19
  643.8 1.8 fusion.62
  645.8 134.5 %all-reduce = (f32[2,1,128]{2,1,0:T(1,128)S(1)}, f32[2,1,128]{2,1,0:T(1,128)S(1)}, f32[128]{0:T(128)S(1)}, f32[128]{0:T(128)S(1)}) all-reduce(f32[2,1,128]{2,1,0:T(1,128)S(1)} %pad_maximum_fusion.10, f32[2,1,128]{2,1,0:T(1,128)S(1)} %pad_maximum_fusion.11, f32[128]{0:T(128)S(1)} %get-tuple-element.7, ...), channel_id=1, replica_groups=mesh['chan'=8,'row'=64] {'row'}, use_global_device_ids=true, to_apply=%region_11.12 | all-reduce | flops 768 | bytes 6144 | tf_op jit(solution)/shard_map/psum | solution.py:161
  780.2 0.6 broadcast_multiply_fusion.1
  780.8 0.6 broadcast_multiply_fusion
  781.4 0.5 broadcast_multiply_fusion.2
  781.9 0.5 broadcast_multiply_fusion.3
  782.4 51.2 %all-reduce.2 = (f32[1,3,448]{2,1,0:T(4,128)S(1)}, f32[1,3,448]{2,1,0:T(4,128)S(1)}) all-reduce(f32[1,3,448]{2,1,0:T(4,128)S(1)} %bitcast.441, f32[1,3,448]{2,1,0:T(4,128)S(1)} %bitcast.442), channel_id=1, replica_groups=mesh['chan'=8,'row'=64] {'chan'}, use_global_device_ids=true, to_apply=%region_7.8 | all-reduce | flops 2688 | bytes 21504 | tf_op jit(solution)/shard_map/psum | solution.py:154
  833.6 1.6 fusion.61
  (62 shorter events, 3.5 us)
Async XLA Ops:
  7.2 1.7 copy-start
  60.0 0.7 copy-start.18
  60.0 0.7 copy-start.22
  63.0 14.5 %copy-start.1 = (bf16[1,3,448,128]{3,2,1,0:T(8,128)(2,1)S(1)}, bf16[1,3,448,128]{3,2,1,0:T(8,128)(2,1)}, u32[]{:S(2)}) copy-start(bf16[1,3,448,128]{3,2,1,0:T(8,128)(2,1)} %param.9) | copy-start | bytes 1032196
  63.0 34.1 %all-to-all-start.1 = ((f32[1,3,2,192,128]{4,2,1,0,3:T(2,128)}), f32[1,3,2,192,128]{4,2,1,0,3:T(2,128)S(1)}, u32[]{:S(2)}, u32[]{:S(2)}) async-start(f32[1,3,2,192,128]{4,2,1,0,3:T(2,128)} %copy.49), calls=%async_computation.1 | async-start | bytes 1179648 | tf_op jit(solution)/shard_map/all_to_all | solution.py:92
  81.9 0.9 copy-start.16
  82.9 0.7 copy-start.17
  97.1 25.0 %all-to-all-start = ((f32[1,3,2,192,128]{4,2,1,0,3:T(2,128)}), f32[1,3,2,192,128]{4,2,1,0,3:T(2,128)}, u32[]{:S(2)}, u32[]{:S(2)}) async-start(f32[1,3,2,192,128]{4,2,1,0,3:T(2,128)} %copy.44), calls=%async_computation | async-start | bytes 1179648 | tf_op jit(solution)/shard_map/all_to_all | solution.py:94
  103.2 0.8 copy-start.6
  105.1 0.7 copy-start.21
  105.8 1.0 copy-start.4
  123.6 0.8 copy-start.7
  123.6 1.0 copy-start.8
  124.4 0.7 copy-start.20
  125.0 0.8 copy-start.5
  125.3 0.7 copy-start.15
  126.4 1.0 copy-start.3
  127.3 0.7 copy-start.14
  129.8 1.0 copy-start.23
  132.3 1.0 copy-start.2
  135.4 5.4 copy-start.9
  135.4 507.6 %all-to-all-start.2 = ((f32[1,192,2,3,128]{4,2,3,0,1:T(2,128)}), f32[1,192,2,3,128]{4,2,3,0,1:T(2,128)S(1)}, u32[]{:S(2)}, u32[]{:S(2)}) async-start(f32[1,192,2,3,128]{4,2,3,0,1:T(2,128)} %copy.54), calls=%async_computation.2 | async-start | bytes 1179648 | tf_op jit(solution)/shard_map/all_to_all | solution.py:149
  140.7 0.8 copy-start.10
  140.7 500.0 %all-reduce.5.cloned.1.call-start = ((), (), s32[]{:S(2)}) async-start(), calls=%async_computation.3 | async-start | bytes 524288 | tf_op jit(solution)/shard_map/psum | solution.py:161
  141.7 0.8 copy-start.11
  142.6 0.8 copy-start.12
  640.7 1.6 copy-start.13
  643.2 0.7 copy-start.19
Sparse Core Ops, SparseCore 0:
  145.1 495.5 all-reduce.4
where the time goes:
time: 843 us; the launch traced here: 842 us
  waiting for transfers between devices  524 us (62%)
  blocking collectives  236 us (28%)
  starting transfers between devices  25.4 us (3%)
  matrix products  15.8 us (2%)
  between operations  14.5 us (2%)
  local copies, waits for them, and re-layouts  13.4 us (2%)
  other arithmetic  13.2 us (2%)
    psum x1, waiting for transfers between devices, on_device(): lax.psum((dw_one, db_one, dw_two, db_two, gain_local, shift_local), 'row')  496 us
    psum x1, blocking collectives, on_device(): lax.psum((dw_one, db_one, dw_two, db_two, gain_local, shift_local), 'row')  134 us
    psum x1, blocking collectives, on_device(): lax.psum((jnp.sum(grad_norm, -1), jnp.sum(grad_norm * normed, -1)), 'chan')  51.2 us
    psum x1, blocking collectives, on_device(): mean = lax.psum(jnp.sum(values, -1), 'chan') / total_chan  26.3 us
    psum x1, blocking collectives, on_device(): variance = lax.psum(jnp.sum(centred * centred, -1), 'chan') / total_chan  24 us
  transfers between devices with their start and end apart: 4, of which 3 were waited for; matrix products, arithmetic and copies ran while one was open for 2% of the time, Pallas kernels for 0%

commit v1 on v0

v1 whole, which is shorter than its diff:
```python
import functools
import math

import jax
import jax.numpy as jnp
import ml_dtypes
import numpy as np
from jax import lax
from jax.experimental import pallas as pl
from jax.experimental.pallas import tpu as pltpu
from jax.sharding import PartitionSpec as P

H = 192
W = 448
K = 192
BS = 128
C = 1024
ROWS = 64
CHANS = 8
HL = H // ROWS
KL = K // ROWS
CHUNK = 2 * HL * KL
LINES = ROWS * CHUNK
PIECE = 9
GLINES = ROWS * PIECE
WPAD = 512

EPS = 1e-05
LAMBDA = 0.01
ROOT_TWO_PI = math.sqrt(2.0 / math.pi)
F32 = jnp.float32
BF16 = jnp.bfloat16
MESH = pl.DeviceIdType.MESH


def halves(table):
    table = table.astype(np.float32)
    high = table.astype(ml_dtypes.bfloat16)
    low = (table - high.astype(np.float32)).astype(ml_dtypes.bfloat16)
    return np.stack([high, low])


def lon_table():
    number = np.arange(K).reshape(ROWS, 1, KL)
    part = np.arange(2).reshape(1, 2, 1)
    number, part = np.broadcast_arrays(number, part)
    number, part = number.reshape(-1, 1), part.reshape(-1, 1)
    phase = (number * np.arange(W)[None, :] % W) * (2.0 * math.pi / W)
    return np.where(part == 0, np.cos(phase), -np.sin(phase)) / math.sqrt(W)


def lat_table():
    q = np.arange(2).reshape(2, 1, 1, 1, 1)
    g = np.arange(H).reshape(1, H, 1, 1, 1)
    hh = np.arange(HL).reshape(1, 1, HL, 1, 1)
    s = np.arange(ROWS).reshape(1, 1, 1, ROWS, 1)
    p = np.arange(2).reshape(1, 1, 1, 1, 2)
    phase = (g * (s * HL + hh) % H) * (2.0 * math.pi / H)
    cosine, sine = np.cos(phase), np.sin(phase)
    table = np.where(q == p, cosine, np.where(q == 0, sine, -sine)) / math.sqrt(H)
    return table.reshape(2 * H, HL * ROWS * 2)


def dot(a, b):
    return lax.dot_general(a, b, (((1,), (0,)), ((), ())), preferred_element_type=F32)


def dot_t(a, b):
    return lax.dot_general(a, b, (((1,), (1,)), ((), ())), preferred_element_type=F32)


def dot_c(a, b):
    return lax.dot_general(a, b, (((0,), (0,)), ((), ())), preferred_element_type=F32)


def split(values):
    high = values.astype(BF16)
    return high, (values - high.astype(F32)).astype(BF16)


def dot3(table, values):
    high, low = split(values)
    return dot(table[0], high) + (dot(table[1], high) + dot(table[0], low))


def gelu_parts(values):
    square = values * values
    tangent = jnp.tanh(ROOT_TWO_PI * (values + 0.044715 * (square * values)))
    plus = 0.5 * (1.0 + tangent)
    slope = plus + 0.5 * values * (1.0 - tangent * tangent) * (
        ROOT_TWO_PI * (1.0 + 3.0 * 0.044715 * square)
    )
    return values * plus, slope


def block_matrix(weight):
    real, imag = weight[0], weight[1]
    return jnp.concatenate(
        [jnp.concatenate([real, imag], 1), jnp.concatenate([-imag, real], 1)], 0
    )


def spread(stats, width):
    high = stats.astype(BF16).astype(F32)
    rest = stats - high
    mid = rest.astype(BF16).astype(F32)
    low = rest - mid
    pieces = jnp.concatenate([high, mid, low, jnp.zeros_like(high)], 0).astype(BF16)
    line = lax.broadcasted_iota(jnp.int32, (32, 2 * HL * BS), 0) % 8
    column = lax.broadcasted_iota(jnp.int32, (32, 2 * HL * BS), 1) // BS
    pick = (line == column).astype(F32).astype(BF16)
    return dot_c(pieces, pick)[:width]


def kernel(
    x_ref, cot_ref, gain_ref, shift_ref, w1_ref, b1_ref, w2_ref, b2_ref,
    lon_ref, lont_ref, lat_ref, latt_ref,
    out_ref, gw1_ref, gb1_ref, gw2_ref, gb2_ref, gg_ref, gs_ref,
    sc, rc, sx, rx, sg, rg, st, rt, su, ru, normed_ref, rstd_ref,
    spec_ref, nspec_ref, hid_ref, slope_ref, factor_ref, gtwo_ref, gpre_ref,
    gw, rw, fold, piece, aw,
    send_sem, recv_sem,
):
    chan = lax.axis_index("chan")
    row = lax.axis_index("row")

    barrier = pltpu.get_barrier_semaphore()

    def greet_row(j, carry):
        pl.semaphore_signal(
            barrier, inc=1, device_id={"row": lax.rem(row + j, ROWS)}, device_id_type=MESH
        )
        return carry

    def greet_chan(j, carry):
        pl.semaphore_signal(
            barrier, inc=1, device_id={"chan": lax.rem(chan + j, CHANS)}, device_id_type=MESH
        )
        return carry

    lax.fori_loop(1, CHANS, greet_chan, 0)
    lax.fori_loop(1, ROWS, greet_row, 0)

    def send_row(source, target, lines, which, same):
        def one(j, carry):
            other = lax.rem(row + j, ROWS)
            block = source if same else source.at[pl.ds(other * lines, lines)]
            pltpu.make_async_remote_copy(
                src_ref=block,
                dst_ref=target.at[pl.ds(row * lines, lines)],
                send_sem=send_sem.at[which],
                recv_sem=recv_sem.at[which],
                device_id={"row": other},
                device_id_type=MESH,
            ).start()
            return carry

        lax.fori_loop(1, ROWS, one, 0)
        own = pl.ds(row * lines, lines)
        pltpu.make_async_copy(
            source if same else source.at[own], target.at[own], recv_sem.at[which]
        ).start()

    def send_chan(source, target, which):
        def one(j, carry):
            pltpu.make_async_remote_copy(
                src_ref=source,
                dst_ref=target.at[chan],
                send_sem=send_sem.at[which],
                recv_sem=recv_sem.at[which],
                device_id={"chan": lax.rem(chan + j, CHANS)},
                device_id_type=MESH,
            ).start()
            return carry

        lax.fori_loop(1, CHANS, one, 0)
        pltpu.make_async_copy(source, target.at[chan], recv_sem.at[which]).start()

    def arrived(target, which):
        pltpu.make_async_copy(target, target, recv_sem.at[which]).wait()

    def left(target, which):
        pltpu.make_async_copy(target, target, send_sem.at[which]).wait()

    ones_wide = jnp.ones((BS, BS), F32).astype(BF16)
    ones_thin = jnp.ones((16, BS), F32).astype(BF16)

    st[...] = jnp.zeros_like(st)
    for h in range(HL):
        block = x_ref[0, h]
        average = dot(block, ones_wide) * (1.0 / BS)
        centred = block.astype(F32) - average
        high, low = split(centred * centred)
        st[h : h + 1, :W] = dot_t(ones_thin, block)[:1]
        st[HL + h : HL + h + 1, :W] = (dot_t(ones_thin, high) + dot_t(ones_thin, low))[:1]
    for h in range(HL):
        block = cot_ref[0, h]
        sc[pl.ds(h, 2 * K, stride=HL), :] = dot(lon_ref[0], block) + dot(lon_ref[1], block)

    pl.semaphore_wait(barrier, ROWS - 1 + CHANS - 1)
    send_chan(st, rt, 0)
    send_row(sc, rc, CHUNK, 1, False)

    arrived(rt, 0)
    total = rt[0]
    for c in range(1, CHANS):
        total = total + rt[c]
    mean = total[:HL] * (1.0 / C)
    squares = total[HL : 2 * HL]
    for c in range(CHANS):
        away = rt[c][:HL] * (1.0 / BS) - mean
        squares = squares + BS * (away * away)
    rstd = lax.rsqrt(squares * (1.0 / C) + EPS)
    wide = spread(jnp.concatenate([mean, rstd, jnp.zeros((2, WPAD), F32)], 0), W)
    for h in range(HL):
        centre = wide[:, h * BS : (h + 1) * BS]
        scale = wide[:, (HL + h) * BS : (HL + h + 1) * BS]
        normed = (x_ref[0, h].astype(F32) - centre) * scale
        normed_ref[h] = normed
        rstd_ref[h] = scale
        sx[pl.ds(h, 2 * K, stride=HL), :] = dot3(lon_ref, normed)
    send_row(sx, rx, CHUNK, 2, False)

    one_matrix = block_matrix(w1_ref)
    two_matrix = block_matrix(w2_ref)
    one_bias = jnp.concatenate([b1_ref[0:1], b1_ref[1:2]], 1)
    two_bias = jnp.concatenate([b2_ref[0:1], b2_ref[1:2]], 1)
    gain = gain_ref[...]
    gain_two = jnp.concatenate([gain, gain], 1)
    shift_two = jnp.concatenate([shift_ref[...] * math.sqrt(H * W), jnp.zeros((1, BS), F32)], 1)
    first = jnp.where(row == 0, 1.0, 0.0).astype(F32)

    def spectrum(landed):
        columns = []
        for k in range(KL):
            columns.append(
                jnp.concatenate(
                    [landed[pl.ds(k * HL + h, 2 * ROWS, stride=HL * KL), :] for h in range(HL)], 0
                )
            )
        return dot3(lat_ref, jnp.concatenate(columns, 1))

    def tokens(values, k):
        block = values[:, k * BS : (k + 1) * BS]
        return jnp.concatenate([block[:H], block[H:]], 1)

    arrived(rx, 2)
    spec = spectrum(rx)
    for k in range(KL):
        plain = tokens(spec, k)
        nspec_ref[k] = plain
        mixed = plain * gain_two
        if k == 0:
            line = lax.broadcasted_iota(jnp.int32, (H, 2 * BS), 0)
            mixed = mixed + jnp.where(line == 0, shift_two * first, 0.0)
        rounded = mixed.astype(BF16)
        spec_ref[k] = rounded
        act, slope = gelu_parts(dot(rounded, one_matrix) + one_bias)
        hidden = act.astype(BF16)
        hid_ref[k] = hidden
        slope_ref[k] = slope
        tangent = jnp.tanh((dot(hidden, two_matrix) + two_bias) / LAMBDA)
        factor_ref[k] = tangent * tangent

    arrived(rc, 1)
    cot_spec = spectrum(rc)
    gain_sum = jnp.zeros((1, 2 * BS), F32)
    one_sum = jnp.zeros((1, 2 * BS), F32)
    two_sum = jnp.zeros((1, 2 * BS), F32)
    columns = []
    for k in range(KL):
        cot_block = tokens(cot_spec, k) * (2.0 - first if k == 0 else 2.0)
        grad_two = (cot_block * factor_ref[k]).astype(BF16)
        gtwo_ref[k] = grad_two
        grad_pre = (dot_t(grad_two, two_matrix) * slope_ref[k]).astype(BF16)
        gpre_ref[k] = grad_pre
        grad_spec = dot_t(grad_pre, one_matrix)
        two_sum = two_sum + jnp.sum(grad_two.astype(F32), 0, keepdims=True)
        one_sum = one_sum + jnp.sum(grad_pre.astype(F32), 0, keepdims=True)
        gain_sum = gain_sum + jnp.sum(grad_spec * nspec_ref[k], 0, keepdims=True)
        if k == 0:
            shift_sum = grad_spec[0:1, :BS] * first
        columns.append(jnp.concatenate([grad_spec[:, :BS], grad_spec[:, BS:]], 0))
    grad_lat = dot3(latt_ref, jnp.concatenate(columns, 1))
    for k in range(KL):
        for h in range(HL):
            sg[pl.ds(k * HL + h, 2 * ROWS, stride=HL * KL), :] = grad_lat[
                h * 2 * ROWS : (h + 1) * 2 * ROWS, k * BS : (k + 1) * BS
            ]
    send_row(sg, rg, CHUNK, 3, False)

    spec_scale = 1.0 / math.sqrt(H * K)
    ln_scale = 1.0 / math.sqrt(H * W)
    for layer, (left_ref, right_ref) in enumerate(((spec_ref, gpre_ref), (hid_ref, gtwo_ref))):
        product = jnp.zeros((2 * BS, 2 * BS), F32)
        for k in range(KL):
            product = product + dot_c(left_ref[k], right_ref[k])
        product = product * spec_scale
        real = product[:BS, :BS] + product[BS:, BS:]
        imag = product[:BS, BS:] - product[BS:, :BS]
        for part, values in enumerate((real, imag)):
            for half in range(2):
                gw[pl.ds(layer * 4 + part * 2 + half, ROWS, stride=PIECE), :] = values[
                    half * ROWS : (half + 1) * ROWS
                ]
    gain_sum = (gain_sum[:, :BS] + gain_sum[:, BS:]) * ln_scale
    gw[pl.ds(PIECE - 1, ROWS, stride=PIECE), :] = jnp.concatenate(
        [
            one_sum[:, :BS] * spec_scale,
            one_sum[:, BS:] * spec_scale,
            two_sum[:, :BS] * spec_scale,
            two_sum[:, BS:] * spec_scale,
            gain_sum,
            shift_sum,
            jnp.zeros((ROWS - 6, BS), F32),
        ],
        0,
    )
    send_row(gw, rw, PIECE, 4, False)

    arrived(rg, 3)
    su[...] = jnp.zeros_like(su)
    grads = []
    for h in range(HL):
        grad_norm = dot3(lont_ref, rg[pl.ds(h, 2 * K, stride=HL), :]) * gain
        high, low = split(grad_norm)
        su[h : h + 1, :W] = (dot_t(ones_thin, high) + dot_t(ones_thin, low))[:1]
        high, low = split(grad_norm * normed_ref[h])
        su[HL + h : HL + h + 1, :W] = (dot_t(ones_thin, high) + dot_t(ones_thin, low))[:1]
        grads.append(grad_norm)
    send_chan(su, ru, 5)

    arrived(rw, 4)
    summed = rw[pl.ds(0, 8 * PIECE), :]
    for s in range(1, ROWS // 8):
        summed = summed + rw[pl.ds(s * 8 * PIECE, 8 * PIECE), :]
    fold[...] = summed
    summed = fold[pl.ds(0, PIECE), :]
    for s in range(1, 8):
        summed = summed + fold[pl.ds(s * PIECE, PIECE), :]
    piece[...] = summed
    send_row(piece, aw, PIECE, 6, True)

    arrived(ru, 5)
    total = ru[0]
    for c in range(1, CHANS):
        total = total + ru[c]
    wide = spread(total * (1.0 / C), W)
    for h in range(HL):
        one = wide[:, h * BS : (h + 1) * BS]
        two = wide[:, (HL + h) * BS : (HL + h + 1) * BS]
        inner = grads[h] - one - normed_ref[h] * two
        out_ref[0, h] = (cot_ref[0, h].astype(F32) + rstd_ref[h] * inner).astype(BF16)

    arrived(aw, 6)
    for layer, target in enumerate((gw1_ref, gw2_ref)):
        for part in range(2):
            for half in range(2):
                target[part, half * ROWS : (half + 1) * ROWS] = aw[
                    pl.ds(layer * 4 + part * 2 + half, ROWS, stride=PIECE), :
                ]
    extras = aw[pl.ds(PIECE - 1, 8, stride=PIECE), :]
    gb1_ref[...] = extras[0:2]
    gb2_ref[...] = extras[2:4]
    gg_ref[...] = extras[4:5]
    gs_ref[...] = extras[5:6]

    left(rt.at[pl.ds(0, CHANS - 1)], 0)
    left(ru.at[pl.ds(0, CHANS - 1)], 5)
    for which in (1, 2, 3):
        left(rc.at[pl.ds(0, LINES - CHUNK)], which)
    for which in (4, 6):
        left(rw.at[pl.ds(0, GLINES - PIECE)], which)


def on_device(
    inputs, cotangent, ln_gain, ln_shift, first_weight, first_bias, second_weight, second_bias
):
    lon = lon_table()
    lat = lat_table()
    tables = [jnp.asarray(halves(t)) for t in (lon, lon.T, lat, lat.T)]
    lines = pltpu.VMEM((LINES, BS), F32)
    glines = pltpu.VMEM((GLINES, BS), F32)
    stats = pltpu.VMEM((8, WPAD), F32)
    landed = pltpu.VMEM((CHANS, 8, WPAD), F32)
    grid = pltpu.VMEM((HL, W, BS), F32)
    wide = pltpu.VMEM((KL, H, 2 * BS), F32)
    narrow = pltpu.VMEM((KL, H, 2 * BS), BF16)
    in_vmem = pl.BlockSpec(memory_space=pltpu.VMEM)
    shape = jax.ShapeDtypeStruct
    outs = pl.pallas_call(
        kernel,
        out_shape=(
            shape((1, HL, W, BS), BF16),
            shape((2, BS, BS), F32),
            shape((2, BS), F32),
            shape((2, BS, BS), F32),
            shape((2, BS), F32),
            shape((1, BS), F32),
            shape((1, BS), F32),
        ),
        in_specs=[in_vmem] * 12,
        out_specs=(in_vmem,) * 7,
        scratch_shapes=[
            lines, lines, lines, lines, lines, lines,
            stats, landed, stats, landed, grid, grid,
            narrow, wide, narrow, wide, wide, narrow, narrow,
            glines, glines, pltpu.VMEM((8 * PIECE, BS), F32), pltpu.VMEM((PIECE, BS), F32), glines,
            pltpu.SemaphoreType.DMA((7,)),
            pltpu.SemaphoreType.DMA((7,)),
        ],
        compiler_params=pltpu.CompilerParams(
            collective_id=0, has_side_effects=True, vmem_limit_bytes=48 * 1024 * 1024
        ),
    )(
        inputs, cotangent, ln_gain.reshape(1, BS), ln_shift.reshape(1, BS),
        first_weight, first_bias, second_weight, second_bias, *tables,
    )
    return outs[:5] + (outs[5].reshape(BS), outs[6].reshape(BS))


def solution(mesh):
    placed = (
        P(None, "row", None, "chan"),
        P(None, "row", None, "chan"),
        P("chan"),
        P("chan"),
        P(None, "chan", None),
        P(None, "chan"),
        P(None, "chan", None),
        P(None, "chan"),
    )
    return jax.shard_map(
        on_device,
        mesh=mesh,
        in_specs=placed,
        out_specs=(
            P(None, "row", None, "chan"),
            P(None, "chan", None),
            P(None, "chan"),
            P(None, "chan", None),
            P(None, "chan"),
            P("chan"),
            P("chan"),
        ),
        check_vma=False,
    )
```

time: 843 us -> 113 us (0.13)
  the two profiles are of different devices: /device:TPU:32 before, /device:TPU:57 now
where the time goes in v1:
time: 113 us
  Pallas kernels  99.2 us (88%)
  local copies, waits for them, and re-layouts  12.9 us (11%)
    pallas_call x1, Pallas kernels, on_device(): pl.pallas_call(kernel, out_shape=(shape((1, HL, W, BS), BF16), shape((2,...  99.2 us
    unnamed x31, local copies, waits for them, and re-layouts  12.9 us

profile of v1, /device:TPU:57, one launch (start us, length us, event | category | flops | bytes accessed | tf_op | source)
XLA Modules:
  0.0 112.7 jit_solution(394627575408650274)
XLA Ops:
  0.6 0.0 copy-start.9
  0.6 0.0 copy-start.11
  0.7 0.0 copy-start.8
  0.7 0.0 copy-start.10
  0.7 0.6 copy-done.9
  1.3 0.0 copy-done.11
  1.3 0.0 copy-done.8
  1.3 0.0 copy-done.10
  1.3 0.0 copy-start
  1.4 1.1 %copy-done = bf16[2,384,448]{2,1,0:T(8,128)(2,1)S(1)} copy-done((bf16[2,384,448]{2,1,0:T(8,128)(2,1)S(1)}, bf16[2,384,448]{2,1,0:T(8,128)(2,1)}, u32[]{:S(2)}) %copy-start) | copy-done | bytes 688152
  2.5 0.0 copy-start.1
  2.5 1.1 copy-done.1
  3.6 0.0 copy-start.2
  3.6 1.1 copy-done.2
  4.6 0.0 copy-start.3
  4.7 1.1 copy-done.3
  5.7 0.0 copy-start.4
  5.7 1.0 copy-done.4
  6.7 0.0 copy-start.5
  6.7 1.0 copy-done.5
  7.7 0.0 copy-start.6
  7.7 0.8 copy-done.6
  8.5 0.0 copy-start.7
  8.5 0.8 copy-done.7
  9.4 99.2 %shard_map.171 = (bf16[1,3,448,128]{3,2,1,0:T(8,128)(2,1)S(1)}, f32[2,128,128]{2,1,0:T(8,128)S(1)}, f32[2,128]{1,0:T(2,128)S(1)}, f32[2,128,128]{2,1,0:T(8,128)S...) custom-call(bf16[1,3,448,128]{3,2,1,0:T(8,128)(2,1)S(1)} %copy-done.4, ...), custom_call_target="tpu_custom_call" | custom-call | tf_op jit(solution)/shard_map/pallas_call | solution.py:391
  108.5 0.7 copy.26
  109.3 0.7 copy.27
  109.9 0.6 copy.28
  110.5 0.7 copy.29
  111.2 0.6 copy.30
  111.7 0.5 copy.31
  112.2 0.5 copy.32
Async XLA Ops:
  0.6 0.7 copy-start.9
  0.6 0.7 copy-start.11
  0.7 0.7 copy-start.8
  0.7 0.7 copy-start.10
  1.3 1.1 %copy-start = (bf16[2,384,448]{2,1,0:T(8,128)(2,1)S(1)}, bf16[2,384,448]{2,1,0:T(8,128)(2,1)}, u32[]{:S(2)}) copy-start(bf16[2,384,448]{2,1,0:T(8,128)(2,1)} %constant.8.clone.lon_ref) | copy-start | bytes 2064388
  2.5 1.1 copy-start.1
  3.6 1.1 copy-start.2
  4.6 1.1 copy-start.3
  5.7 1.0 copy-start.4
  6.7 1.0 copy-start.5
  7.7 0.8 copy-start.6
  8.5 0.8 copy-start.7

commit v2 on v1

v2 whole, which is shorter than its diff:
```python
import math

import jax
import jax.numpy as jnp
import ml_dtypes
import numpy as np
from jax import lax
from jax.experimental import pallas as pl
from jax.experimental.pallas import tpu as pltpu
from jax.sharding import PartitionSpec as P

H = 192
W = 448
K = 192
BS = 128
C = 1024
ZS, YS, CORES = 8, 4, 2
ROWS = ZS * YS * CORES
CHIPS = ZS * YS
XS = 4
CHANS = 2 * XS
HL = H // ROWS
KL = K // ROWS
CHUNK = 2 * HL
LINES = ROWS * CHUNK
PIECE = 9
GLINES = CHIPS * PIECE
WT = -(-W // BS)
SLINES = 2 * HL * WT

EPS = 1e-05
LAMBDA = 0.01
ROOT_TWO_PI = math.sqrt(2.0 / math.pi)
F32 = jnp.float32
BF16 = jnp.bfloat16
MESH = pl.DeviceIdType.MESH
COT, MIXED, GRAD = 0, KL, 2 * KL
STATS, SUMS, SWAP, SCATTER, GATHER, JOIN = (3 * KL + i for i in (0, 2, 4, 5, 6, 7))
SEMS = 3 * KL + 8


def halves(table):
    table = table.astype(np.float32)
    high = table.astype(ml_dtypes.bfloat16)
    low = (table - high.astype(np.float32)).astype(ml_dtypes.bfloat16)
    return np.stack([high, low])


def lon_table():
    kk = np.arange(KL).reshape(KL, 1, 1)
    owner = np.arange(ROWS).reshape(1, ROWS, 1)
    part = np.arange(2).reshape(1, 1, 2)
    number, part = np.broadcast_arrays(owner * KL + kk, part)
    number, part = number.reshape(-1, 1), part.reshape(-1, 1)
    phase = (number * np.arange(W)[None, :] % W) * (2.0 * math.pi / W)
    return np.where(part == 0, np.cos(phase), -np.sin(phase)) / math.sqrt(W)


def lat_table():
    q = np.arange(2).reshape(2, 1, 1, 1, 1)
    g = np.arange(H).reshape(1, H, 1, 1, 1)
    hh = np.arange(HL).reshape(1, 1, HL, 1, 1)
    s = np.arange(ROWS).reshape(1, 1, 1, ROWS, 1)
    p = np.arange(2).reshape(1, 1, 1, 1, 2)
    phase = (g * (s * HL + hh) % H) * (2.0 * math.pi / H)
    cosine, sine = np.cos(phase), np.sin(phase)
    table = np.where(q == p, cosine, np.where(q == 0, sine, -sine)) / math.sqrt(H)
    return table.reshape(2 * H, HL * ROWS * 2)


def lon_back_table():
    high, low = halves(lon_table())
    cut = lambda t: t.reshape(KL, 2 * ROWS, W).transpose(0, 2, 1)
    return np.concatenate([cut(high), cut(low), cut(high)], 2)


def dot(a, b):
    return lax.dot_general(a, b, (((1,), (0,)), ((), ())), preferred_element_type=F32)


def dot_t(a, b):
    return lax.dot_general(a, b, (((1,), (1,)), ((), ())), preferred_element_type=F32)


def dot_c(a, b):
    return lax.dot_general(a, b, (((0,), (0,)), ((), ())), preferred_element_type=F32)


def split(values):
    high = values.astype(BF16)
    return high, (values - high.astype(F32)).astype(BF16)


def dot3(table_high, table_low, values):
    high, low = split(values)
    return dot(table_high, high) + (dot(table_low, high) + dot(table_high, low))


def gelu_parts(values):
    square = values * values
    tangent = jnp.tanh(ROOT_TWO_PI * (values + 0.044715 * (square * values)))
    plus = 0.5 * (1.0 + tangent)
    slope = plus + 0.5 * values * (1.0 - tangent * tangent) * (
        ROOT_TWO_PI * (1.0 + 3.0 * 0.044715 * square)
    )
    return values * plus, slope


def block_matrix(weight):
    real, imag = weight[0], weight[1]
    return jnp.concatenate(
        [jnp.concatenate([real, imag], 1), jnp.concatenate([-imag, real], 1)], 0
    )


def diagonal(rows):
    return (
        lax.broadcasted_iota(jnp.int32, (rows, BS), 0)
        == lax.broadcasted_iota(jnp.int32, (rows, BS), 1)
    )


def pack(values):
    lines = []
    for t in range(WT):
        block = values[t * BS : min((t + 1) * BS, W)]
        lines.append(jnp.sum(jnp.where(diagonal(block.shape[0]), block, 0.0), 0, keepdims=True))
    return jnp.concatenate(lines, 0)


def spread(turned, line):
    blocks = []
    for t in range(WT):
        column = turned[: min(BS, W - t * BS), line + t : line + t + 1]
        blocks.append(jnp.broadcast_to(column, (column.shape[0], BS)))
    return jnp.concatenate(blocks, 0)


def kernel(*refs):
    sources, refs = refs[:12], refs[12:]
    held, refs = refs[-12:], refs[:-12]
    on_chip(sources, held, *held, *refs)


def on_chip(
    sources, held,
    cot_ref, lon_ref, x_ref, gain_ref, shift_ref, w1_ref, b1_ref, w2_ref, b2_ref,
    lat_ref, latt_ref, lont_ref,
    out_hbm, gw1_hbm, gb1_hbm, gw2_hbm, gb2_hbm, gg_hbm, gs_hbm,
    sc, rc, sx, rx, sg, rg, st, rt, su, ru, normed_ref, rstd_ref, grad_ref,
    dw_ref, gw, gx, hw, rw, fold, piece, aw,
    send_sem, recv_sem, load_sem, store_sem,
    out_ref, gw1_ref, gb1_ref, gw2_ref, gb2_ref, gg_ref, gs_ref,
):
    chan = lax.axis_index("chan")
    row = lax.axis_index("row")
    z, y, core = row // (YS * CORES), row // CORES % YS, row % CORES
    chip = row // CORES
    along_x = chan % XS
    chan_base = chan - along_x
    opposite = lax.rem(chan + XS, CHANS)
    twin = row + 1 - 2 * core

    def peer(i):
        other_z = lax.rem(z + i % ZS, ZS)
        other_y = lax.rem(y + i // (ZS * CORES), YS)
        other_core = lax.rem(core + i // ZS, CORES)
        return (other_z * YS + other_y) * CORES + other_core

    def peer_chip(i):
        return lax.rem(z + i % ZS, ZS) * YS + lax.rem(y + i // ZS, YS)

    def peer_x(i):
        return chan_base + lax.rem(along_x + i, XS)

    barrier = pltpu.get_barrier_semaphore()

    def greet(name, other):
        pl.semaphore_signal(barrier, inc=1, device_id={name: other}, device_id_type=MESH)

    def greet_row(i, carry):
        greet("row", peer(i))
        return carry

    lax.fori_loop(1, ROWS, greet_row, 0)
    for i in range(1, XS):
        greet("chan", peer_x(i))
    greet("chan", opposite)

    loads = [
        pltpu.make_async_copy(source, target, load_sem.at[i])
        for i, (source, target) in enumerate(zip(sources, held))
    ]
    for load in loads:
        load.start()

    def remote(source, target, which, name, other):
        return pltpu.make_async_remote_copy(
            src_ref=source,
            dst_ref=target,
            send_sem=send_sem.at[which],
            recv_sem=recv_sem.at[which],
            device_id={name: other},
            device_id_type=MESH,
        )

    def arrived(target, which):
        pltpu.make_async_copy(target, target, recv_sem.at[which]).wait()

    def left(target, which):
        pltpu.make_async_copy(target, target, send_sem.at[which]).wait()

    own = pl.ds(row * CHUNK, CHUNK)
    own_piece = pl.ds(chip * PIECE, PIECE)

    def send_chunks(source, target, k, which):
        def one(i, carry):
            other = peer(i)
            block = source.at[k, pl.ds(other * CHUNK, CHUNK)]
            remote(block, target.at[k, own], which + k, "row", other).start()
            return carry

        lax.fori_loop(1, ROWS, one, 0)
        pltpu.make_async_copy(
            source.at[k, own], target.at[k, own], recv_sem.at[which + k]
        ).start()

    for load in loads[:3]:
        load.wait()

    ones = jnp.ones((BS, BS), F32).astype(BF16)
    for h in range(HL):
        block = x_ref[0, h]
        amount = dot(block, ones)
        centred = block.astype(F32) - amount * (1.0 / BS)
        high, low = split(centred * centred)
        st[0, pl.ds(h * WT, WT), :] = pack(amount)
        st[0, pl.ds((HL + h) * WT, WT), :] = pack(dot(high, ones) + dot(low, ones))

    cot_wide = jnp.concatenate([cot_ref[0, h] for h in range(HL)], 1)

    def transform(k, product):
        rows = pl.ds(k * 2 * ROWS, 2 * ROWS)
        return product(lon_ref[0, rows, :], lon_ref[1, rows, :])

    def lay(target, k, values):
        for h in range(HL):
            target[k, pl.ds(h, 2 * ROWS, stride=HL), :] = values[:, h * BS : (h + 1) * BS]

    def cot_lon(k):
        lay(sc, k, transform(k, lambda high, low: dot(high, cot_wide) + dot(low, cot_wide)))

    cot_lon(0)

    pl.semaphore_wait(barrier, ROWS - 1 + XS)

    for i in range(1, XS):
        remote(st.at[0], rt.at[along_x], STATS, "chan", peer_x(i)).start()
    send_chunks(sc, rc, 0, COT)
    cot_lon(1)
    cot_lon(2)

    arrived(rt.at[pl.ds(0, XS - 1)], STATS)
    mine = st[0]

    def part(i):
        return jnp.where(along_x == i, mine, rt[i])

    parts = [part(i) for i in range(XS)]
    half = SLINES // 2
    amount = parts[0][:half] + parts[1][:half] + parts[2][:half] + parts[3][:half]
    squares = parts[0][half:] + parts[1][half:] + parts[2][half:] + parts[3][half:]
    average = amount * (1.0 / (XS * BS))
    for i in range(XS):
        away = parts[i][:half] * (1.0 / BS) - average
        squares = squares + BS * (away * away)
    st[1] = jnp.concatenate([amount, squares], 0)
    remote(st.at[1], rt.at[XS], STATS + 1, "chan", opposite).start()

    send_chunks(sc, rc, 1, COT)

    arrived(rt.at[XS], STATS + 1)
    amount_two = rt[XS, pl.ds(0, half), :]
    mean = (amount + amount_two) * (1.0 / C)
    away = average - mean
    away_two = amount_two * (1.0 / (XS * BS)) - mean
    squares = squares + rt[XS, pl.ds(half, half), :] + (XS * BS) * (
        away * away + away_two * away_two
    )
    rstd = lax.rsqrt(squares * (1.0 / C) + EPS)

    turned = jnp.concatenate([mean, rstd], 0).T
    for h in range(HL):
        scale = spread(turned, half + h * WT)
        normed_ref[:, h * BS : (h + 1) * BS] = (
            x_ref[0, h].astype(F32) - spread(turned, h * WT)
        ) * scale
        rstd_ref[:, h * BS : (h + 1) * BS] = scale
    high, low = split(normed_ref[...])

    def mixed_lon(k):
        lay(sx, k, transform(k, lambda a, b: dot(a, high) + (dot(b, high) + dot(a, low))))

    mixed_lon(0)
    send_chunks(sx, rx, 0, MIXED)
    mixed_lon(1)
    send_chunks(sx, rx, 1, MIXED)
    send_chunks(sc, rc, 2, COT)
    mixed_lon(2)
    send_chunks(sx, rx, 2, MIXED)

    for load in loads[3:]:
        load.wait()
    one_matrix = block_matrix(w1_ref)
    two_matrix = block_matrix(w2_ref)
    one_bias = jnp.concatenate([b1_ref[0:1], b1_ref[1:2]], 1)
    two_bias = jnp.concatenate([b2_ref[0:1], b2_ref[1:2]], 1)
    gain = gain_ref[...]
    gain_two = jnp.concatenate([gain, gain], 1)
    shift_two = jnp.concatenate([shift_ref[...] * math.sqrt(H * W), jnp.zeros((1, BS), F32)], 1)
    first = jnp.where(row == 0, 1.0, 0.0).astype(F32)
    spec_scale = 1.0 / math.sqrt(H * K)
    ln_scale = 1.0 / math.sqrt(H * W)

    def gathered(landed, k):
        return jnp.concatenate(
            [landed[k, pl.ds(h, 2 * ROWS, stride=HL), :] for h in range(HL)], 0
        )

    def tokens(values):
        return jnp.concatenate([values[:H], values[H:]], 1)

    gain_sum = jnp.zeros((1, 2 * BS), F32)
    one_sum = jnp.zeros((1, 2 * BS), F32)
    two_sum = jnp.zeros((1, 2 * BS), F32)
    for k in range(KL):
        arrived(rc.at[k], COT + k)
        arrived(rx.at[k], MIXED + k)
        both = dot3(
            lat_ref[0], lat_ref[1], jnp.concatenate([gathered(rx, k), gathered(rc, k)], 1)
        )
        plain = tokens(both[:, :BS])
        mixed = plain * gain_two
        if k == 0:
            line = lax.broadcasted_iota(jnp.int32, (H, 2 * BS), 0)
            mixed = mixed + jnp.where(line == 0, shift_two * first, 0.0)
        rounded = mixed.astype(BF16)
        act, slope = gelu_parts(dot(rounded, one_matrix) + one_bias)
        hidden = act.astype(BF16)
        tangent = jnp.tanh((dot(hidden, two_matrix) + two_bias) * (1.0 / LAMBDA))
        cot_block = tokens(both[:, BS:]) * (2.0 - first if k == 0 else 2.0)
        grad_two = (cot_block * (tangent * tangent)).astype(BF16)
        grad_pre = (dot_t(grad_two, two_matrix) * slope).astype(BF16)
        grad_spec = dot_t(grad_pre, one_matrix)
        grad_lat = dot3(
            latt_ref[0], latt_ref[1],
            jnp.concatenate([grad_spec[:, :BS], grad_spec[:, BS:]], 0),
        )
        for h in range(HL):
            sg[k, pl.ds(h, 2 * ROWS, stride=HL), :] = grad_lat[h * 2 * ROWS : (h + 1) * 2 * ROWS]
        if k < KL - 1:
            send_chunks(sg, rg, k, GRAD)
        two_sum = two_sum + jnp.sum(grad_two.astype(F32), 0, keepdims=True)
        one_sum = one_sum + jnp.sum(grad_pre.astype(F32), 0, keepdims=True)
        gain_sum = gain_sum + jnp.sum(grad_spec * plain, 0, keepdims=True)
        if k == 0:
            shift_sum = grad_spec[0:1, :BS] * first
        for layer, (before, after) in enumerate(((rounded, grad_pre), (hidden, grad_two))):
            product = dot_c(before, after)
            dw_ref[layer] = product if k == 0 else dw_ref[layer] + product

    for layer in range(2):
        product = dw_ref[layer] * spec_scale
        real = product[:BS, :BS] + product[BS:, BS:]
        imag = product[:BS, BS:] - product[BS:, :BS]
        for part_index, values in enumerate((real, imag)):
            for c in range(CORES):
                for sub in range(2):
                    start = (c * 2 + sub) * CHIPS
                    gw[c, pl.ds(layer * 4 + part_index * 2 + sub, CHIPS, stride=PIECE), :] = (
                        values[start : start + CHIPS]
                    )
    gain_sum = (gain_sum[:, :BS] + gain_sum[:, BS:]) * ln_scale
    gw[0, pl.ds(PIECE - 1, CHIPS, stride=PIECE), :] = jnp.concatenate(
        [
            one_sum[:, :BS] * spec_scale,
            one_sum[:, BS:] * spec_scale,
            two_sum[:, :BS] * spec_scale,
            two_sum[:, BS:] * spec_scale,
            gain_sum,
            shift_sum,
            jnp.zeros((CHIPS - 6, BS), F32),
        ],
        0,
    )
    gw[1, pl.ds(PIECE - 1, CHIPS, stride=PIECE), :] = jnp.zeros((CHIPS, BS), F32)
    remote(gw.at[1 - core], gx, SWAP, "row", twin).start()
    arrived(gx, SWAP)
    hw[...] = gw[core] + gx[...]

    def scatter(i, carry):
        other = peer_chip(i)
        block = hw.at[pl.ds(other * PIECE, PIECE)]
        remote(block, rw.at[own_piece], SCATTER, "row", other * CORES + core).start()
        return carry

    lax.fori_loop(1, CHIPS, scatter, 0)
    pltpu.make_async_copy(hw.at[own_piece], rw.at[own_piece], recv_sem.at[SCATTER]).start()
    send_chunks(sg, rg, KL - 1, GRAD)

    def lon_back(k):
        values = jnp.concatenate(
            [rg[k, pl.ds(h, 2 * ROWS, stride=HL), :] for h in range(HL)], 1
        )
        high, low = split(values)
        return dot(lont_ref[k], jnp.concatenate([high, high, low], 0))

    arrived(rg.at[0], GRAD)
    grad_ref[...] = lon_back(0)
    arrived(rg.at[1], GRAD + 1)
    grad_ref[...] = grad_ref[...] + lon_back(1)

    arrived(rw, SCATTER)
    slab = 8 * PIECE
    summed = rw[pl.ds(0, slab), :]
    for s in range(1, CHIPS // 8):
        summed = summed + rw[pl.ds(s * slab, slab), :]
    fold[...] = summed
    summed = fold[pl.ds(0, PIECE), :]
    for s in range(1, 8):
        summed = summed + fold[pl.ds(s * PIECE, PIECE), :]
    piece[...] = summed

    def gather(i, carry):
        other = peer_chip(i)
        remote(piece, aw.at[core, own_piece], GATHER, "row", other * CORES + core).start()
        return carry

    lax.fori_loop(1, CHIPS, gather, 0)
    pltpu.make_async_copy(piece, aw.at[core, own_piece], recv_sem.at[GATHER]).start()

    arrived(rg.at[2], GRAD + 2)
    zeros = jnp.zeros((BS, BS), F32).astype(BF16)
    pair = jnp.concatenate(
        [jnp.concatenate([ones, zeros], 1), jnp.concatenate([zeros, ones], 1)], 0
    )
    gain_wide = jnp.concatenate([gain] * HL, 1)
    grad_ref[...] = (grad_ref[...] + lon_back(2)) * gain_wide
    for h in range(HL):
        grad_norm = grad_ref[:, h * BS : (h + 1) * BS]
        product = grad_norm * normed_ref[:, h * BS : (h + 1) * BS]
        sums = dot(jnp.concatenate([grad_norm.astype(BF16), product.astype(BF16)], 1), pair)
        su[0, pl.ds(h * WT, WT), :] = pack(sums[:, :BS])
        su[0, pl.ds((HL + h) * WT, WT), :] = pack(sums[:, BS:])
    for i in range(1, XS):
        remote(su.at[0], ru.at[along_x], SUMS, "chan", peer_x(i)).start()
    arrived(ru.at[pl.ds(0, XS - 1)], SUMS)
    mine = su[0]
    total = jnp.where(along_x == 0, mine, ru[0])
    for i in range(1, XS):
        total = total + jnp.where(along_x == i, mine, ru[i])
    su[1] = total
    remote(su.at[1], ru.at[XS], SUMS + 1, "chan", opposite).start()

    arrived(aw.at[core], GATHER)
    remote(aw.at[core], aw.at[core], JOIN, "row", twin).start()

    arrived(ru.at[XS], SUMS + 1)
    turned = ((total + ru[XS]) * (1.0 / C)).T
    stores = []
    for h in range(HL):
        lanes = slice(h * BS, (h + 1) * BS)
        inner = grad_ref[:, lanes] - spread(turned, h * WT) - normed_ref[:, lanes] * spread(
            turned, half + h * WT
        )
        out_ref[0, h] = (cot_ref[0, h].astype(F32) + rstd_ref[:, lanes] * inner).astype(BF16)
        stores.append(pltpu.make_async_copy(out_ref.at[0, h], out_hbm.at[0, h], store_sem.at[h]))
        stores[-1].start()

    arrived(aw.at[1 - core], JOIN)
    for layer, target in enumerate((gw1_ref, gw2_ref)):
        for part_index in range(2):
            for c in range(CORES):
                for sub in range(2):
                    start = (c * 2 + sub) * CHIPS
                    target[part_index, start : start + CHIPS] = aw[
                        c, pl.ds(layer * 4 + part_index * 2 + sub, CHIPS, stride=PIECE), :
                    ]
    extras = aw[0, pl.ds(PIECE - 1, 8, stride=PIECE), :]
    gb1_ref[...] = extras[0:2]
    gb2_ref[...] = extras[2:4]
    gg_ref[...] = extras[4:5]
    gs_ref[...] = extras[5:6]
    for i, (source, target) in enumerate(
        (
            (gw1_ref, gw1_hbm), (gb1_ref, gb1_hbm), (gw2_ref, gw2_hbm),
            (gb2_ref, gb2_hbm), (gg_ref, gg_hbm), (gs_ref, gs_hbm),
        )
    ):
        stores.append(pltpu.make_async_copy(source, target, store_sem.at[HL + i]))
        stores[-1].start()

    for which in (STATS, SUMS):
        left(rt.at[pl.ds(0, XS - 1)], which)
        left(rt.at[XS], which + 1)
    for k in range(KL):
        for which in (COT, MIXED, GRAD):
            left(rc.at[0, pl.ds(0, LINES - CHUNK)], which + k)
    for which in (SWAP, JOIN):
        left(hw, which)
    for which in (SCATTER, GATHER):
        left(hw.at[pl.ds(0, GLINES - PIECE)], which)
    for store in stores:
        store.wait()


def hand_out(*refs):
    given, wanted, held = refs[:7], refs[7:14], refs[14:21]
    in_sem, out_sem = refs[21:]
    brought = [pltpu.make_async_copy(given[i], held[i], in_sem.at[i]) for i in range(7)]
    taken = [pltpu.make_async_copy(held[i], wanted[i], out_sem.at[i]) for i in range(7)]
    for copy in brought:
        copy.start()
    for first, second in zip(brought, taken):
        first.wait()
        second.start()
    for copy in taken:
        copy.wait()


def on_device(
    inputs, cotangent, ln_gain, ln_shift, first_weight, first_bias, second_weight, second_bias
):
    lat = lat_table()
    lon, lat, latt, lont = (
        jnp.asarray(t)
        for t in (halves(lon_table()), halves(lat), halves(lat.T), lon_back_table())
    )
    sources = (
        cotangent, lon, inputs, ln_gain.reshape(1, BS), ln_shift.reshape(1, BS),
        first_weight, first_bias, second_weight, second_bias, lat, latt, lont,
    )
    lines = pltpu.VMEM((KL, LINES, BS), F32)
    glines = pltpu.VMEM((GLINES, BS), F32)
    stats = pltpu.VMEM((2, SLINES, BS), F32)
    landed = pltpu.VMEM((XS + 1, SLINES, BS), F32)
    grid = pltpu.VMEM((W, HL * BS), F32)
    shape = jax.ShapeDtypeStruct
    results = (
        shape((1, HL, W, BS), BF16),
        shape((2, BS, BS), F32),
        shape((2, BS), F32),
        shape((2, BS, BS), F32),
        shape((2, BS), F32),
        shape((1, BS), F32),
        shape((1, BS), F32),
    )
    in_hbm = pl.BlockSpec(memory_space=pltpu.HBM)
    outs = pl.pallas_call(
        kernel,
        out_shape=results,
        in_specs=[in_hbm] * 12,
        out_specs=(in_hbm,) * 7,
        scratch_shapes=[
            lines, lines, lines, lines, lines, lines,
            stats, landed, stats, landed, grid, grid, grid,
            pltpu.VMEM((2, 2 * BS, 2 * BS), F32),
            pltpu.VMEM((CORES, GLINES, BS), F32), glines, glines, glines,
            pltpu.VMEM((8 * PIECE, BS), F32), pltpu.VMEM((PIECE, BS), F32),
            pltpu.VMEM((CORES, GLINES, BS), F32),
            pltpu.SemaphoreType.DMA((SEMS,)),
            pltpu.SemaphoreType.DMA((SEMS,)),
            pltpu.SemaphoreType.DMA((12,)),
            pltpu.SemaphoreType.DMA((HL + 6,)),
        ]
        + [pltpu.VMEM(r.shape, r.dtype) for r in results]
        + [pltpu.VMEM(source.shape, source.dtype) for source in sources],
        compiler_params=pltpu.CompilerParams(
            collective_id=0, has_side_effects=True, vmem_limit_bytes=64 * 1024 * 1024
        ),
    )(*sources)
    outs = pl.pallas_call(
        hand_out,
        out_shape=results,
        in_specs=[in_hbm] * 7,
        out_specs=(in_hbm,) * 7,
        scratch_shapes=[pltpu.VMEM(r.shape, r.dtype) for r in results]
        + [pltpu.SemaphoreType.DMA((7,))] * 2,
        compiler_params=pltpu.CompilerParams(vmem_limit_bytes=64 * 1024 * 1024),
    )(*outs)
    return tuple(outs[:5]) + (outs[5].reshape(BS), outs[6].reshape(BS))


def solution(mesh):
    placed = (
        P(None, "row", None, "chan"),
        P(None, "row", None, "chan"),
        P("chan"),
        P("chan"),
        P(None, "chan", None),
        P(None, "chan"),
        P(None, "chan", None),
        P(None, "chan"),
    )
    return jax.shard_map(
        on_device,
        mesh=mesh,
        in_specs=placed,
        out_specs=(
            P(None, "row", None, "chan"),
            P(None, "chan", None),
            P(None, "chan"),
            P(None, "chan", None),
            P(None, "chan"),
            P("chan"),
            P("chan"),
        ),
        check_vma=False,
    )
```

time: 113 us -> 78.6 us (0.70)
  Pallas kernels: 99.2 us -> 77.2 us
  local copies, waits for them, and re-layouts: 12.9 us -> 0 us
    pallas_call x1 -> x2, Pallas kernels: 99.2 us -> 77.2 us  [the longest x1 75.2 us: on_device(): pl.pallas_call(kernel, out_shape=results, in_specs=[in_hbm] * 12, out_spe...]
    unnamed x31 -> x0, local copies, waits for them, and re-layouts: 12.9 us -> none
where the time goes in v2:
time: 78.6 us; the launch traced here: 77.8 us
  Pallas kernels  77.2 us (98%)
    pallas_call x1, Pallas kernels, on_device(): pl.pallas_call(kernel, out_shape=results, in_specs=[in_hbm] * 12, out_spe...  75.2 us
    pallas_call x1, Pallas kernels, on_device(): pl.pallas_call(hand_out, out_shape=results, in_specs=[in_hbm] * 7, out_sp...  1.92 us

profile of v2, /device:TPU:57, one launch (start us, length us, event | category | flops | bytes accessed | tf_op | source)
XLA Modules:
  0.0 77.8 jit_solution(1684139901960228168)
XLA Ops:
  0.6 75.2 %shard_map.171 = (bf16[1,3,448,128]{3,2,1,0:T(8,128)(2,1)}, f32[2,128,128]{2,1,0:T(8,128)}, f32[2,128]{1,0:T(2,128)}, f32[2,128,128]{2,1,0:T(8,128)}, f32[2,128]...) custom-call(bf16[1,3,448,128]{3,2,1,0:T(8,128)(2,1)} %refs_0_.1, bf16[2,384,448]{2,1,0:T(8,128)(2,1)} %constant.8.clone.refs_1_, ...), custom_call_target="tpu_custom_call" | custom-call | tf_op jit(solution)/shard_map/pallas_call | solution.py:559
  75.9 1.9 %shard_map.172 = (bf16[1,3,448,128]{3,2,1,0:T(8,128)(2,1)}, f32[2,128,128]{2,1,0:T(8,128)}, f32[2,128]{1,0:T(2,128)}, f32[2,128,128]{2,1,0:T(8,128)}, f32[2,128]...) custom-call(bf16[1,3,448,128]{3,2,1,0:T(8,128)(2,1)} %get-tuple-element.21.refs_0_, ...), custom_call_target="tpu_custom_call" | custom-call | tf_op jit(solution)/shard_map/pallas_call | solution.py:582

commit v3 on v2

--- a/solution.py
+++ b/solution.py
@@ -146,11 +146,10 @@
     sources, held,
     cot_ref, lon_ref, x_ref, gain_ref, shift_ref, w1_ref, b1_ref, w2_ref, b2_ref,
     lat_ref, latt_ref, lont_ref,
-    out_hbm, gw1_hbm, gb1_hbm, gw2_hbm, gb2_hbm, gg_hbm, gs_hbm,
+    out_ref, gw1_ref, gb1_ref, gw2_ref, gb2_ref, gg_ref, gs_ref,
     sc, rc, sx, rx, sg, rg, st, rt, su, ru, normed_ref, rstd_ref, grad_ref,
     dw_ref, gw, gx, hw, rw, fold, piece, aw,
-    send_sem, recv_sem, load_sem, store_sem,
-    out_ref, gw1_ref, gb1_ref, gw2_ref, gb2_ref, gg_ref, gs_ref,
+    send_sem, recv_sem, load_sem,
 ):
     chan = lax.axis_index("chan")
     row = lax.axis_index("row")
@@ -161,38 +160,50 @@
     opposite = lax.rem(chan + XS, CHANS)
     twin = row + 1 - 2 * core
 
-    def peer(i):
-        other_z = lax.rem(z + i % ZS, ZS)
-        other_y = lax.rem(y + i // (ZS * CORES), YS)
-        other_core = lax.rem(core + i // ZS, CORES)
-        return (other_z * YS + other_y) * CORES + other_core
-
-    def peer_chip(i):
-        return lax.rem(z + i % ZS, ZS) * YS + lax.rem(y + i // ZS, YS)
+    ahead = [lax.rem(z + i, ZS) for i in range(ZS)]
+    row_of = [a * (YS * CORES) for a in ahead]
+    chip_of = [a * YS for a in ahead]
+
+    def each_row(act, steps=tuple(range(ZS))):
+        def level(i, carry):
+            base = lax.rem(y + i // CORES, YS) * CORES + lax.rem(core + i, CORES)
+            for step in steps:
+                act(row_of[step] + base)
+            return carry
+
+        for step in steps:
+            if step:
+                act(row_of[step] + y * CORES + core)
+        lax.fori_loop(1, YS * CORES, level, 0)
+
+    def each_chip(act):
+        def level(i, carry):
+            base = lax.rem(y + i, YS)
+            for offset in chip_of:
+                act(offset + base)
+            return carry
+
+        for offset in chip_of[1:]:
+            act(offset + y)
+        lax.fori_loop(1, YS, level, 0)
 
     def peer_x(i):
         return chan_base + lax.rem(along_x + i, XS)
-
-    barrier = pltpu.get_barrier_semaphore()
-
-    def greet(name, other):
-        pl.semaphore_signal(barrier, inc=1, device_id={name: other}, device_id_type=MESH)
-
-    def greet_row(i, carry):
-        greet("row", peer(i))
-        return carry
-
-    lax.fori_loop(1, ROWS, greet_row, 0)
-    for i in range(1, XS):
-        greet("chan", peer_x(i))
-    greet("chan", opposite)
 
     loads = [
         pltpu.make_async_copy(source, target, load_sem.at[i])
         for i, (source, target) in enumerate(zip(sources, held))
     ]
-    for load in loads:
+    for load in loads[:3]:
         load.start()
+    barrier = pltpu.get_barrier_semaphore()
+
+    def greet(name, other):
+        pl.semaphore_signal(barrier, inc=1, device_id={name: other}, device_id_type=MESH)
+
+    for i in range(1, CHANS):
+        greet("chan", lax.rem(chan + i, CHANS))
+    each_row(lambda other: greet("row", other), (4, 3, 5, 2, 6, 1, 7, 0))
 
     def remote(source, target, which, name, other):
         return pltpu.make_async_remote_copy(
@@ -214,20 +225,33 @@
     own_piece = pl.ds(chip * PIECE, PIECE)
 
     def send_chunks(source, target, k, which):
-        def one(i, carry):
-            other = peer(i)
+        def one(other):
             block = source.at[k, pl.ds(other * CHUNK, CHUNK)]
             remote(block, target.at[k, own], which + k, "row", other).start()
-            return carry
-
-        lax.fori_loop(1, ROWS, one, 0)
+
+        each_row(one)
         pltpu.make_async_copy(
             source.at[k, own], target.at[k, own], recv_sem.at[which + k]
         ).start()
 
-    for load in loads[:3]:
+    for load in loads[:2]:
         load.wait()
-
+    cot_wide = jnp.concatenate([cot_ref[0, h] for h in range(HL)], 1)
+
+    def transform(k, product):
+        rows = pl.ds(k * 2 * ROWS, 2 * ROWS)
+        return product(lon_ref[0, rows, :], lon_ref[1, rows, :])
+
+    def lay(target, k, values):
+        for h in range(HL):
+            target[k, pl.ds(h, 2 * ROWS, stride=HL), :] = values[:, h * BS : (h + 1) * BS]
+
+    def cot_lon(k):
+        lay(sc, k, transform(k, lambda high, low: dot(high, cot_wide) + dot(low, cot_wide)))
+
+    cot_lon(0)
+
+    loads[2].wait()
     ones = jnp.ones((BS, BS), F32).astype(BF16)
     for h in range(HL):
         block = x_ref[0, h]
@@ -236,23 +260,7 @@
         high, low = split(centred * centred)
         st[0, pl.ds(h * WT, WT), :] = pack(amount)
         st[0, pl.ds((HL + h) * WT, WT), :] = pack(dot(high, ones) + dot(low, ones))
-
-    cot_wide = jnp.concatenate([cot_ref[0, h] for h in range(HL)], 1)
-
-    def transform(k, product):
-        rows = pl.ds(k * 2 * ROWS, 2 * ROWS)
-        return product(lon_ref[0, rows, :], lon_ref[1, rows, :])
-
-    def lay(target, k, values):
-        for h in range(HL):
-            target[k, pl.ds(h, 2 * ROWS, stride=HL), :] = values[:, h * BS : (h + 1) * BS]
-
-    def cot_lon(k):
-        lay(sc, k, transform(k, lambda high, low: dot(high, cot_wide) + dot(low, cot_wide)))
-
-    cot_lon(0)
-
-    pl.semaphore_wait(barrier, ROWS - 1 + XS)
+    pl.semaphore_wait(barrier, ROWS - 1 + CHANS - 1)
 
     for i in range(1, XS):
         remote(st.at[0], rt.at[along_x], STATS, "chan", peer_x(i)).start()
@@ -278,6 +286,9 @@
     remote(st.at[1], rt.at[XS], STATS + 1, "chan", opposite).start()
 
     send_chunks(sc, rc, 1, COT)
+    send_chunks(sc, rc, 2, COT)
+    for load in loads[3:]:
+        load.start()
 
     arrived(rt.at[XS], STATS + 1)
     amount_two = rt[XS, pl.ds(0, half), :]
@@ -305,7 +316,6 @@
     send_chunks(sx, rx, 0, MIXED)
     mixed_lon(1)
     send_chunks(sx, rx, 1, MIXED)
-    send_chunks(sc, rc, 2, COT)
     mixed_lon(2)
     send_chunks(sx, rx, 2, MIXED)
 
@@ -398,13 +408,11 @@
     arrived(gx, SWAP)
     hw[...] = gw[core] + gx[...]
 
-    def scatter(i, carry):
-        other = peer_chip(i)
+    def scatter(other):
         block = hw.at[pl.ds(other * PIECE, PIECE)]
         remote(block, rw.at[own_piece], SCATTER, "row", other * CORES + core).start()
-        return carry
-
-    lax.fori_loop(1, CHIPS, scatter, 0)
+
+    each_chip(scatter)
     pltpu.make_async_copy(hw.at[own_piece], rw.at[own_piece], recv_sem.at[SCATTER]).start()
     send_chunks(sg, rg, KL - 1, GRAD)
 
@@ -431,12 +439,10 @@
         summed = summed + fold[pl.ds(s * PIECE, PIECE), :]
     piece[...] = summed
 
-    def gather(i, carry):
-        other = peer_chip(i)
+    def gather(other):
         remote(piece, aw.at[core, own_piece], GATHER, "row", other * CORES + core).start()
-        return carry
-
-    lax.fori_loop(1, CHIPS, gather, 0)
+
+    each_chip(gather)
     pltpu.make_async_copy(piece, aw.at[core, own_piece], recv_sem.at[GATHER]).start()
 
     arrived(rg.at[2], GRAD + 2)
@@ -450,32 +456,26 @@
         grad_norm = grad_ref[:, h * BS : (h + 1) * BS]
         product = grad_norm * normed_ref[:, h * BS : (h + 1) * BS]
         sums = dot(jnp.concatenate([grad_norm.astype(BF16), product.astype(BF16)], 1), pair)
-        su[0, pl.ds(h * WT, WT), :] = pack(sums[:, :BS])
-        su[0, pl.ds((HL + h) * WT, WT), :] = pack(sums[:, BS:])
-    for i in range(1, XS):
-        remote(su.at[0], ru.at[along_x], SUMS, "chan", peer_x(i)).start()
-    arrived(ru.at[pl.ds(0, XS - 1)], SUMS)
-    mine = su[0]
-    total = jnp.where(along_x == 0, mine, ru[0])
-    for i in range(1, XS):
-        total = total + jnp.where(along_x == i, mine, ru[i])
-    su[1] = total
-    remote(su.at[1], ru.at[XS], SUMS + 1, "chan", opposite).start()
+        su[pl.ds(h * WT, WT), :] = pack(sums[:, :BS])
+        su[pl.ds((HL + h) * WT, WT), :] = pack(sums[:, BS:])
+    for i in range(1, CHANS):
+        remote(su, ru.at[chan], SUMS, "chan", lax.rem(chan + i, CHANS)).start()
+    pltpu.make_async_copy(su, ru.at[chan], recv_sem.at[SUMS]).start()
 
     arrived(aw.at[core], GATHER)
     remote(aw.at[core], aw.at[core], JOIN, "row", twin).start()
 
-    arrived(ru.at[XS], SUMS + 1)
-    turned = ((total + ru[XS]) * (1.0 / C)).T
-    stores = []
+    arrived(ru, SUMS)
+    total = ru[0]
+    for i in range(1, CHANS):
+        total = total + ru[i]
+    turned = (total * (1.0 / C)).T
     for h in range(HL):
         lanes = slice(h * BS, (h + 1) * BS)
         inner = grad_ref[:, lanes] - spread(turned, h * WT) - normed_ref[:, lanes] * spread(
             turned, half + h * WT
         )
         out_ref[0, h] = (cot_ref[0, h].astype(F32) + rstd_ref[:, lanes] * inner).astype(BF16)
-        stores.append(pltpu.make_async_copy(out_ref.at[0, h], out_hbm.at[0, h], store_sem.at[h]))
-        stores[-1].start()
 
     arrived(aw.at[1 - core], JOIN)
     for layer, target in enumerate((gw1_ref, gw2_ref)):
@@ -491,18 +491,10 @@
     gb2_ref[...] = extras[2:4]
     gg_ref[...] = extras[4:5]
     gs_ref[...] = extras[5:6]
-    for i, (source, target) in enumerate(
-        (
-            (gw1_ref, gw1_hbm), (gb1_ref, gb1_hbm), (gw2_ref, gw2_hbm),
-            (gb2_ref, gb2_hbm), (gg_ref, gg_hbm), (gs_ref, gs_hbm),
-        )
-    ):
-        stores.append(pltpu.make_async_copy(source, target, store_sem.at[HL + i]))
-        stores[-1].start()
-
-    for which in (STATS, SUMS):
-        left(rt.at[pl.ds(0, XS - 1)], which)
-        left(rt.at[XS], which + 1)
+
+    left(rt.at[pl.ds(0, XS - 1)], STATS)
+    left(rt.at[XS], STATS + 1)
+    left(ru.at[pl.ds(0, CHANS - 1)], SUMS)
     for k in range(KL):
         for which in (COT, MIXED, GRAD):
             left(rc.at[0, pl.ds(0, LINES - CHUNK)], which + k)
@@ -510,21 +502,14 @@
         left(hw, which)
     for which in (SCATTER, GATHER):
         left(hw.at[pl.ds(0, GLINES - PIECE)], which)
-    for store in stores:
-        store.wait()
 
 
 def hand_out(*refs):
-    given, wanted, held = refs[:7], refs[7:14], refs[14:21]
-    in_sem, out_sem = refs[21:]
-    brought = [pltpu.make_async_copy(given[i], held[i], in_sem.at[i]) for i in range(7)]
-    taken = [pltpu.make_async_copy(held[i], wanted[i], out_sem.at[i]) for i in range(7)]
-    for copy in brought:
+    sem = refs[14]
+    copies = [pltpu.make_async_copy(refs[i], refs[7 + i], sem.at[i]) for i in range(7)]
+    for copy in copies:
         copy.start()
-    for first, second in zip(brought, taken):
-        first.wait()
-        second.start()
-    for copy in taken:
+    for copy in copies:
         copy.wait()
 
 
@@ -542,8 +527,6 @@
     )
     lines = pltpu.VMEM((KL, LINES, BS), F32)
     glines = pltpu.VMEM((GLINES, BS), F32)
-    stats = pltpu.VMEM((2, SLINES, BS), F32)
-    landed = pltpu.VMEM((XS + 1, SLINES, BS), F32)
     grid = pltpu.VMEM((W, HL * BS), F32)
     shape = jax.ShapeDtypeStruct
     results = (
@@ -555,15 +538,18 @@
         shape((1, BS), F32),
         shape((1, BS), F32),
     )
+    in_vmem = pl.BlockSpec(memory_space=pltpu.VMEM)
     in_hbm = pl.BlockSpec(memory_space=pltpu.HBM)
     outs = pl.pallas_call(
         kernel,
-        out_shape=results,
+        out_shape=tuple(pltpu.VMEM(r.shape, r.dtype) for r in results),
         in_specs=[in_hbm] * 12,
-        out_specs=(in_hbm,) * 7,
+        out_specs=(in_vmem,) * 7,
         scratch_shapes=[
             lines, lines, lines, lines, lines, lines,
-            stats, landed, stats, landed, grid, grid, grid,
+            pltpu.VMEM((2, SLINES, BS), F32), pltpu.VMEM((XS + 1, SLINES, BS), F32),
+            pltpu.VMEM((SLINES, BS), F32), pltpu.VMEM((CHANS, SLINES, BS), F32),
+            grid, grid, grid,
             pltpu.VMEM((2, 2 * BS, 2 * BS), F32),
             pltpu.VMEM((CORES, GLINES, BS), F32), glines, glines, glines,
             pltpu.VMEM((8 * PIECE, BS), F32), pltpu.VMEM((PIECE, BS), F32),
@@ -571,23 +557,19 @@
             pltpu.SemaphoreType.DMA((SEMS,)),
             pltpu.SemaphoreType.DMA((SEMS,)),
             pltpu.SemaphoreType.DMA((12,)),
-            pltpu.SemaphoreType.DMA((HL + 6,)),
         ]
-        + [pltpu.VMEM(r.shape, r.dtype) for r in results]
         + [pltpu.VMEM(source.shape, source.dtype) for source in sources],
         compiler_params=pltpu.CompilerParams(
-            collective_id=0, has_side_effects=True, vmem_limit_bytes=64 * 1024 * 1024
+            collective_id=0, has_side_effects=True, vmem_limit_bytes=60 * 1024 * 1024
         ),
     )(*sources)
     outs = pl.pallas_call(
         hand_out,
         out_shape=results,
-        in_specs=[in_hbm] * 7,
+        in_specs=[in_vmem] * 7,
         out_specs=(in_hbm,) * 7,
-        scratch_shapes=[pltpu.VMEM(r.shape, r.dtype) for r in results]
-        + [pltpu.SemaphoreType.DMA((7,))] * 2,
-        compiler_params=pltpu.CompilerParams(vmem_limit_bytes=64 * 1024 * 1024),
-    )(*outs)
+        scratch_shapes=[pltpu.SemaphoreType.DMA((7,))],
+    )(*[pltpu.with_memory_space_constraint(o, pltpu.VMEM) for o in outs])
     return tuple(outs[:5]) + (outs[5].reshape(BS), outs[6].reshape(BS))
 
 

time: 78.6 us -> 71.7 us (0.912)
  the two profiles are of different devices: /device:TPU:57 before, /device:TPU:8 now
where the time goes in v3:
time: 71.7 us; the launch traced here: 71.6 us
  Pallas kernels  71 us (99%)
    pallas_call x1, Pallas kernels, on_device(): pl.pallas_call(kernel, out_shape=tuple((pltpu.VMEM(r.shape, r.dtype) for...  70.1 us

profile of v3, /device:TPU:8, one launch (start us, length us, event | category | flops | bytes accessed | tf_op | source)
XLA Modules:
  0.0 71.6 jit_solution(11811911527988452249)
XLA Ops:
  0.6 70.1 %shard_map.171 = (bf16[1,3,448,128]{3,2,1,0:T(8,128)(2,1)S(1)}, f32[2,128,128]{2,1,0:T(8,128)S(1)}, f32[2,128]{1,0:T(2,128)S(1)}, f32[2,128,128]{2,1,0:T(8,128)S...) custom-call(bf16[1,3,448,128]{3,2,1,0:T(8,128)(2,1)} %refs_0_.1, ...), custom_call_target="tpu_custom_call" | custom-call | tf_op jit(solution)/shard_map/pallas_call | solution.py:543
  70.7 0.9 %shard_map.172 = (bf16[1,3,448,128]{3,2,1,0:T(8,128)(2,1)}, f32[2,128,128]{2,1,0:T(8,128)}, f32[2,128]{1,0:T(2,128)}, f32[2,128,128]{2,1,0:T(8,128)}, f32[2,128]...) custom-call(bf16[1,3,448,128]{3,2,1,0:T(8,128)(2,1)S(1)} %get-tuple-element.21.refs_0_, ...), custom_call_target="tpu_custom_call" | custom-call | tf_op jit(solution)/shard_map/pallas_call | solution.py:566

commit v4 on v3

--- a/solution.py
+++ b/solution.py
@@ -69,9 +69,8 @@
 
 
 def lon_back_table():
-    high, low = halves(lon_table())
-    cut = lambda t: t.reshape(KL, 2 * ROWS, W).transpose(0, 2, 1)
-    return np.concatenate([cut(high), cut(low), cut(high)], 2)
+    table = halves(lon_table())[0].reshape(KL, 2 * ROWS, W).transpose(0, 2, 1)
+    return np.concatenate([table, table], 2)
 
 
 def dot(a, b):
@@ -94,6 +93,13 @@
 def dot3(table_high, table_low, values):
     high, low = split(values)
     return dot(table_high, high) + (dot(table_low, high) + dot(table_high, low))
+
+
+def dot2(table, values):
+    high, low = split(values)
+    both = dot(table, jnp.concatenate([high, low], 1))
+    width = values.shape[1]
+    return both[:, :width] + both[:, width:]
 
 
 def gelu_parts(values):
@@ -147,7 +153,7 @@
     cot_ref, lon_ref, x_ref, gain_ref, shift_ref, w1_ref, b1_ref, w2_ref, b2_ref,
     lat_ref, latt_ref, lont_ref,
     out_ref, gw1_ref, gb1_ref, gw2_ref, gb2_ref, gg_ref, gs_ref,
-    sc, rc, sx, rx, sg, rg, st, rt, su, ru, normed_ref, rstd_ref, grad_ref,
+    sc, rc, sx, rx, sg, rg, st, rt, su, ru, normed_ref, rstd_ref, grad_ref, cot_spec_ref,
     dw_ref, gw, gx, hw, rw, fold, piece, aw,
     send_sem, recv_sem, load_sem,
 ):
@@ -345,11 +351,16 @@
     two_sum = jnp.zeros((1, 2 * BS), F32)
     for k in range(KL):
         arrived(rc.at[k], COT + k)
+    cot_spec = dot3(
+        lat_ref[0], lat_ref[1], jnp.concatenate([gathered(rc, k) for k in range(KL)], 1)
+    )
+    for k in range(KL):
+        block = tokens(cot_spec[:, k * BS : (k + 1) * BS])
+        cot_spec_ref[k] = block * (2.0 - first if k == 0 else 2.0)
+    for k in range(KL):
         arrived(rx.at[k], MIXED + k)
-        both = dot3(
-            lat_ref[0], lat_ref[1], jnp.concatenate([gathered(rx, k), gathered(rc, k)], 1)
-        )
-        plain = tokens(both[:, :BS])
+        values = gathered(rx, k)
+        plain = tokens(dot2(lat_ref[0], values) + dot(lat_ref[1], values.astype(BF16)))
         mixed = plain * gain_two
         if k == 0:
             line = lax.broadcasted_iota(jnp.int32, (H, 2 * BS), 0)
@@ -358,13 +369,11 @@
         act, slope = gelu_parts(dot(rounded, one_matrix) + one_bias)
         hidden = act.astype(BF16)
         tangent = jnp.tanh((dot(hidden, two_matrix) + two_bias) * (1.0 / LAMBDA))
-        cot_block = tokens(both[:, BS:]) * (2.0 - first if k == 0 else 2.0)
-        grad_two = (cot_block * (tangent * tangent)).astype(BF16)
+        grad_two = (cot_spec_ref[k] * (tangent * tangent)).astype(BF16)
         grad_pre = (dot_t(grad_two, two_matrix) * slope).astype(BF16)
         grad_spec = dot_t(grad_pre, one_matrix)
-        grad_lat = dot3(
-            latt_ref[0], latt_ref[1],
-            jnp.concatenate([grad_spec[:, :BS], grad_spec[:, BS:]], 0),
+        grad_lat = dot2(
+            latt_ref[...], jnp.concatenate([grad_spec[:, :BS], grad_spec[:, BS:]], 0)
         )
         for h in range(HL):
             sg[k, pl.ds(h, 2 * ROWS, stride=HL), :] = grad_lat[h * 2 * ROWS : (h + 1) * 2 * ROWS]
@@ -421,7 +430,7 @@
             [rg[k, pl.ds(h, 2 * ROWS, stride=HL), :] for h in range(HL)], 1
         )
         high, low = split(values)
-        return dot(lont_ref[k], jnp.concatenate([high, high, low], 0))
+        return dot(lont_ref[k], jnp.concatenate([high, low], 0))
 
     arrived(rg.at[0], GRAD)
     grad_ref[...] = lon_back(0)
@@ -462,6 +471,12 @@
         remote(su, ru.at[chan], SUMS, "chan", lax.rem(chan + i, CHANS)).start()
     pltpu.make_async_copy(su, ru.at[chan], recv_sem.at[SUMS]).start()
 
+    for h in range(HL):
+        lanes = slice(h * BS, (h + 1) * BS)
+        scale = rstd_ref[:, lanes]
+        grad_ref[:, lanes] = cot_ref[0, h].astype(F32) + scale * grad_ref[:, lanes]
+        normed_ref[:, lanes] = scale * normed_ref[:, lanes]
+
     arrived(aw.at[core], GATHER)
     remote(aw.at[core], aw.at[core], JOIN, "row", twin).start()
 
@@ -472,10 +487,11 @@
     turned = (total * (1.0 / C)).T
     for h in range(HL):
         lanes = slice(h * BS, (h + 1) * BS)
-        inner = grad_ref[:, lanes] - spread(turned, h * WT) - normed_ref[:, lanes] * spread(
-            turned, half + h * WT
-        )
-        out_ref[0, h] = (cot_ref[0, h].astype(F32) + rstd_ref[:, lanes] * inner).astype(BF16)
+        out_ref[0, h] = (
+            grad_ref[:, lanes]
+            - rstd_ref[:, lanes] * spread(turned, h * WT)
+            - normed_ref[:, lanes] * spread(turned, half + h * WT)
+        ).astype(BF16)
 
     arrived(aw.at[1 - core], JOIN)
     for layer, target in enumerate((gw1_ref, gw2_ref)):
@@ -519,7 +535,7 @@
     lat = lat_table()
     lon, lat, latt, lont = (
         jnp.asarray(t)
-        for t in (halves(lon_table()), halves(lat), halves(lat.T), lon_back_table())
+        for t in (halves(lon_table()), halves(lat), halves(lat.T)[0], lon_back_table())
     )
     sources = (
         cotangent, lon, inputs, ln_gain.reshape(1, BS), ln_shift.reshape(1, BS),
@@ -549,7 +565,7 @@
             lines, lines, lines, lines, lines, lines,
             pltpu.VMEM((2, SLINES, BS), F32), pltpu.VMEM((XS + 1, SLINES, BS), F32),
             pltpu.VMEM((SLINES, BS), F32), pltpu.VMEM((CHANS, SLINES, BS), F32),
-            grid, grid, grid,
+            grid, grid, grid, pltpu.VMEM((KL, H, 2 * BS), F32),
             pltpu.VMEM((2, 2 * BS, 2 * BS), F32),
             pltpu.VMEM((CORES, GLINES, BS), F32), glines, glines, glines,
             pltpu.VMEM((8 * PIECE, BS), F32), pltpu.VMEM((PIECE, BS), F32),

time: 71.7 us -> 71.1 us (level)
  no operation moved by 1% of the time
where the time goes in v4:
time: 71.1 us; the launch traced here: 71 us
  Pallas kernels  70.4 us (99%)
    pallas_call x1, Pallas kernels, on_device(): pl.pallas_call(kernel, out_shape=tuple((pltpu.VMEM(r.shape, r.dtype) for...  69.5 us

profile of v4, /device:TPU:8, one launch (start us, length us, event | category | flops | bytes accessed | tf_op | source)
XLA Modules:
  0.0 71.0 jit_solution(11600030294341274032)
XLA Ops:
  0.6 69.5 %shard_map.171 = (bf16[1,3,448,128]{3,2,1,0:T(8,128)(2,1)S(1)}, f32[2,128,128]{2,1,0:T(8,128)S(1)}, f32[2,128]{1,0:T(2,128)S(1)}, f32[2,128,128]{2,1,0:T(8,128)S...) custom-call(bf16[1,3,448,128]{3,2,1,0:T(8,128)(2,1)} %refs_0_.1, ...), custom_call_target="tpu_custom_call" | custom-call | tf_op jit(solution)/shard_map/pallas_call | solution.py:559
  70.1 0.9 %shard_map.172 = (bf16[1,3,448,128]{3,2,1,0:T(8,128)(2,1)}, f32[2,128,128]{2,1,0:T(8,128)}, f32[2,128]{1,0:T(2,128)}, f32[2,128,128]{2,1,0:T(8,128)}, f32[2,128]...) custom-call(bf16[1,3,448,128]{3,2,1,0:T(8,128)(2,1)S(1)} %get-tuple-element.21.refs_0_, ...), custom_call_target="tpu_custom_call" | custom-call | tf_op jit(solution)/shard_map/pallas_call | solution.py:582

commit v5 on v4

--- a/solution.py
+++ b/solution.py
@@ -346,6 +346,11 @@
     def tokens(values):
         return jnp.concatenate([values[:H], values[H:]], 1)
 
+    def back(k, values):
+        values = dot2(latt_ref[...], jnp.concatenate([values[:, :BS], values[:, BS:]], 0))
+        for h in range(HL):
+            sg[k, pl.ds(h, 2 * ROWS, stride=HL), :] = values[h * 2 * ROWS : (h + 1) * 2 * ROWS]
+
     gain_sum = jnp.zeros((1, 2 * BS), F32)
     one_sum = jnp.zeros((1, 2 * BS), F32)
     two_sum = jnp.zeros((1, 2 * BS), F32)
@@ -372,12 +377,8 @@
         grad_two = (cot_spec_ref[k] * (tangent * tangent)).astype(BF16)
         grad_pre = (dot_t(grad_two, two_matrix) * slope).astype(BF16)
         grad_spec = dot_t(grad_pre, one_matrix)
-        grad_lat = dot2(
-            latt_ref[...], jnp.concatenate([grad_spec[:, :BS], grad_spec[:, BS:]], 0)
-        )
-        for h in range(HL):
-            sg[k, pl.ds(h, 2 * ROWS, stride=HL), :] = grad_lat[h * 2 * ROWS : (h + 1) * 2 * ROWS]
         if k < KL - 1:
+            back(k, grad_spec)
             send_chunks(sg, rg, k, GRAD)
         two_sum = two_sum + jnp.sum(grad_two.astype(F32), 0, keepdims=True)
         one_sum = one_sum + jnp.sum(grad_pre.astype(F32), 0, keepdims=True)
@@ -414,6 +415,7 @@
     )
     gw[1, pl.ds(PIECE - 1, CHIPS, stride=PIECE), :] = jnp.zeros((CHIPS, BS), F32)
     remote(gw.at[1 - core], gx, SWAP, "row", twin).start()
+    back(KL - 1, grad_spec)
     arrived(gx, SWAP)
     hw[...] = gw[core] + gx[...]
 
@@ -522,7 +524,15 @@
 
 def hand_out(*refs):
     sem = refs[14]
-    copies = [pltpu.make_async_copy(refs[i], refs[7 + i], sem.at[i]) for i in range(7)]
+    pairs = [(refs[i], refs[7 + i]) for i in range(1, 7)]
+    for h in range(HL):
+        for start in range(0, W, W // 2):
+            rows = pl.ds(start, W // 2)
+            pairs.insert(0, (refs[0].at[0, h, rows], refs[7].at[0, h, rows]))
+    copies = [
+        pltpu.make_async_copy(source, target, sem.at[i])
+        for i, (source, target) in enumerate(pairs)
+    ]
     for copy in copies:
         copy.start()
     for copy in copies:
@@ -584,7 +594,7 @@
         out_shape=results,
         in_specs=[in_vmem] * 7,
         out_specs=(in_hbm,) * 7,
-        scratch_shapes=[pltpu.SemaphoreType.DMA((7,))],
+        scratch_shapes=[pltpu.SemaphoreType.DMA((2 * HL + 6,))],
     )(*[pltpu.with_memory_space_constraint(o, pltpu.VMEM) for o in outs])
     return tuple(outs[:5]) + (outs[5].reshape(BS), outs[6].reshape(BS))
 

time: 71.1 us -> 71.1 us (level)
  the two profiles are of different devices: /device:TPU:8 before, /device:TPU:57 now
where the time goes in v5:
time: 71.1 us; the launch traced here: 69.7 us
  Pallas kernels  69.1 us (97%)
    pallas_call x1, Pallas kernels, on_device(): pl.pallas_call(kernel, out_shape=tuple((pltpu.VMEM(r.shape, r.dtype) for...  68.1 us

profile of v5, /device:TPU:57, one launch (start us, length us, event | category | flops | bytes accessed | tf_op | source)
XLA Modules:
  0.0 69.7 jit_solution(14849969472162191896)
XLA Ops:
  0.6 68.1 %shard_map.171 = (bf16[1,3,448,128]{3,2,1,0:T(8,128)(2,1)S(1)}, f32[2,128,128]{2,1,0:T(8,128)S(1)}, f32[2,128]{1,0:T(2,128)S(1)}, f32[2,128,128]{2,1,0:T(8,128)S...) custom-call(bf16[1,3,448,128]{3,2,1,0:T(8,128)(2,1)} %refs_0_.1, ...), custom_call_target="tpu_custom_call" | custom-call | tf_op jit(solution)/shard_map/pallas_call | solution.py:569
  68.8 0.9 %shard_map.172 = (bf16[1,3,448,128]{3,2,1,0:T(8,128)(2,1)}, f32[2,128,128]{2,1,0:T(8,128)}, f32[2,128]{1,0:T(2,128)}, f32[2,128,128]{2,1,0:T(8,128)}, f32[2,128]...) custom-call(bf16[1,3,448,128]{3,2,1,0:T(8,128)(2,1)S(1)} %get-tuple-element.21.refs_0_, ...), custom_call_target="tpu_custom_call" | custom-call | tf_op jit(solution)/shard_map/pallas_call | solution.py:592
